TPU v7x, 32 devices: a whole 2x2x4 slice. The times are simulated.
32 devices in a mesh: groups: 1, cells: 8 (over z, y), ctx: 4 (over x, core), dp: 1.
Axes of the slice: x: 2, y: 2, z: 4, core: 2. Of those that a mesh axis runs over, the one named last changes fastest.
Arguments:
- cell_feats: bfloat16 [1, 32768, 128], P(('groups', 'dp'), ('cells', 'ctx')), may hold values from -8 to 8
- cell_types: int32 [1, 256], P(('groups', 'dp'), ('cells', 'ctx')), may hold values from 0 to 3
- cell_routes: int32 [1, 32768, 2], P(('groups', 'dp'), ('cells', 'ctx')), may hold values from -1 to 127, as said below
- positions: float32 [1, 3, 4096], P(('groups', 'dp'), None, ('cells', 'ctx')), may hold values from -1 to 1
- targets: float32 [1, 4, 4096], P(('groups', 'dp'), None, ('cells', 'ctx')), may hold values from -6 to 6
- type_weight: bfloat16 [4, 128, 768], replicated, may hold values from -0.5 to 0.5
- query_weight: bfloat16 [768, 768], replicated, may hold values from -0.21875 to 0.21875
- key_weight: bfloat16 [768, 768], replicated, may hold values from -0.21875 to 0.21875
- out_weight: bfloat16 [768, 4], replicated, may hold values from -0.21875 to 0.21875
- anchor_gain: float32 [768], replicated, may hold values from 0.5 to 2
- query_gain: float32 [768], replicated, may hold values from 0.5 to 2
- key_gain: float32 [768], replicated, may hold values from 0.5 to 2
Outputs:
- prediction: float32 [1, 4, 4096], P(('groups', 'dp'), None, ('cells', 'ctx'))
- grad_query: float32 [768, 768], P(('groups', 'cells'), ('ctx', 'dp'))
Inputs may be any that keep to these rules, and one draw needn't show every extreme that they name: `cell_routes`: A car's cells form 8 x 4 aligned tiles of 1024 rows; tile j lies in slab j // 4 and column j % 4, and supernode s belongs to tile s // 4. An entry is -1, a supernode of its own cell's tile, or a supernode of a tile in the same column and another slab. At most 32 entries of one tile name supernodes of one other tile; in every car the tiles of some slab receive exactly 32 such entries from every other tile of their column.
All inputs are finite; a program needn't handle non-finite values.
Results may differ from a plain program's by a relative error of at most 0.013.
Values may be sent and summed in bfloat16 or wider, within the bound.
A program may use at most 64 MiB of HBM per device.

v0:
```python
import functools
import math

import jax
import jax.numpy as jnp
from jax import lax
from jax.experimental import pallas as pl
from jax.experimental.pallas import tpu as pltpu
from jax.sharding import PartitionSpec as P

D = 768
HEAD_DIM = 64
SN_DEV = 4
FREQ = 128


EPS = 1e-06


def head_norm(values):
    shaped = values.reshape(values.shape[:-1] + (values.shape[-1] // HEAD_DIM, HEAD_DIM))
    inverse = lax.rsqrt(jnp.mean(shaped * shaped, axis=-1, keepdims=True) + EPS)
    return (shaped * inverse).reshape(values.shape)


def embed_positions(coords):
    freq_ids = jnp.arange(FREQ, dtype=jnp.float32)
    rate_table = math.pi * jnp.exp2(freq_ids * (6.0 / FREQ))
    angles = jnp.transpose(coords)[:, :, None] * rate_table[None, None, :]
    sin_cos = jnp.stack([jnp.sin(angles), jnp.cos(angles)], axis=2)
    return sin_cos.reshape(coords.shape[1], 6 * FREQ).astype(jnp.bfloat16)


def cell_embed(cell_rows, type_ids, type_weight):
    row_count = cell_rows.shape[0]
    per_block = row_count // type_ids.shape[0]
    shaped = cell_rows.reshape(type_ids.shape[0], per_block, cell_rows.shape[1])
    chosen = type_weight[0][None]
    for type_id in range(1, type_weight.shape[0]):
        chosen = jnp.where((type_ids == type_id)[:, None, None], type_weight[type_id][None], chosen)
    pre_act = jnp.einsum("bnf,bfd->bnd", shaped, chosen, preferred_element_type=jnp.float32)
    return jnp.tanh(pre_act).astype(jnp.bfloat16).reshape(row_count, -1)


def make_keys(anchors, key_weight, key_gain):
    key_lin = jnp.dot(anchors, key_weight, preferred_element_type=jnp.float32)
    return (head_norm(key_lin) * key_gain).astype(jnp.bfloat16)


def general_device(
    cell_feats,
    cell_types,
    cell_routes,
    positions,
    targets,
    type_weight,
    query_weight,
    key_weight,
    out_weight,
    anchor_gain,
    query_gain,
    key_gain,
):
    slab_count = lax.axis_size("cells")
    column_count = lax.axis_size("ctx")
    cell_rows = cell_feats[0]
    type_ids = cell_types[0]
    routes = cell_routes[0]
    embedded = cell_embed(cell_rows, type_ids, type_weight)
    slots = jnp.arange(slab_count * SN_DEV, dtype=jnp.int32)
    owned = (slots // SN_DEV * column_count + lax.axis_index("ctx")) * SN_DEV + slots % SN_DEV
    table = jnp.sum((routes[None, :, :] == owned[:, None, None]).astype(jnp.int32), axis=2)
    partial = jnp.dot(table.astype(jnp.bfloat16), embedded, preferred_element_type=jnp.float32)
    pooled = lax.psum_scatter(partial, "cells", scatter_dimension=0, tiled=True)
    inverse = lax.rsqrt(jnp.mean(pooled * pooled, axis=-1, keepdims=True) + EPS)
    anchors = (pooled * inverse * anchor_gain).astype(jnp.bfloat16)
    own_keys = make_keys(anchors, key_weight, key_gain)
    all_keys, all_anchors = (
        lax.all_gather(own_keys, ("cells", "ctx"), axis=0, tiled=True),
        lax.all_gather(anchors, ("cells", "ctx"), axis=0, tiled=True),
    )
    embed = embed_positions(positions[0])
    query_lin = jnp.dot(embed, query_weight, preferred_element_type=jnp.float32)
    query_hat = (head_norm(query_lin) * query_gain).astype(jnp.bfloat16)
    query_count = embed.shape[0]
    head_count = D // HEAD_DIM
    group_size = 4
    score_scale = HEAD_DIM ** (-0.5)
    query_heads = query_hat.reshape(query_count, head_count, HEAD_DIM)
    key_heads = all_keys.reshape(-1, head_count, HEAD_DIM)
    value_heads = all_anchors.reshape(-1, head_count, HEAD_DIM)
    probs_saved = []
    outputs = []
    for first_head in range(0, head_count, group_size):
        last_head = first_head + group_size
        scores = (
            jnp.einsum(
                "qhd,khd->hqk",
                query_heads[:, first_head:last_head],
                key_heads[:, first_head:last_head],
                preferred_element_type=jnp.float32,
            )
            * score_scale
        )
        exponent = jnp.exp(scores)
        probs_f32 = exponent / jnp.sum(exponent, axis=-1, keepdims=True)
        probs_saved.append(probs_f32)
        outputs.append(
            jnp.einsum(
                "hqk,khd->qhd",
                probs_f32.astype(jnp.bfloat16),
                value_heads[:, first_head:last_head],
                preferred_element_type=jnp.float32,
            )
        )
    attended = jnp.concatenate(outputs, axis=1).reshape(query_count, D).astype(jnp.bfloat16)
    predicted = lax.dot_general(
        out_weight, attended, (((0,), (1,)), ((), ())), preferred_element_type=jnp.float32
    )
    residue = predicted - targets[0]
    grad_attended = lax.dot_general(
        residue,
        out_weight.astype(jnp.float32),
        (((0,), (1,)), ((), ())),
        precision=lax.Precision.HIGHEST,
    ).astype(jnp.bfloat16)
    grad_heads = grad_attended.reshape(query_count, head_count, HEAD_DIM)
    pieces = []
    for group_index, first_head in enumerate(range(0, head_count, group_size)):
        last_head = first_head + group_size
        probs_f32 = probs_saved[group_index]
        grad_weights = jnp.einsum(
            "qhd,khd->hqk",
            grad_heads[:, first_head:last_head],
            value_heads[:, first_head:last_head],
            preferred_element_type=jnp.float32,
        )
        grad_scores = probs_f32 * (
            grad_weights - jnp.sum(probs_f32 * grad_weights, axis=-1, keepdims=True)
        )
        pieces.append(
            jnp.einsum(
                "hqk,khd->qhd",
                grad_scores.astype(jnp.bfloat16),
                key_heads[:, first_head:last_head],
                preferred_element_type=jnp.float32,
            )
            * score_scale
        )
    grad_qhat = jnp.concatenate(pieces, axis=1).reshape(query_count, D)
    weighted = (grad_qhat * query_gain).reshape(query_count, head_count, HEAD_DIM)
    shaped = query_lin.reshape(query_count, head_count, HEAD_DIM)
    norm_inverse = lax.rsqrt(jnp.mean(shaped * shaped, axis=-1, keepdims=True) + EPS)
    unit_rows = shaped * norm_inverse
    grad_qlin = (
        (
            (weighted - unit_rows * jnp.mean(weighted * unit_rows, axis=-1, keepdims=True))
            * norm_inverse
        )
        .reshape(query_count, D)
        .astype(jnp.bfloat16)
    )
    summed = lax.psum_scatter(
        lax.dot_general(
            embed, grad_qlin, (((0,), (0,)), ((), ())), preferred_element_type=jnp.float32
        ),
        "cells",
        scatter_dimension=0,
        tiled=True,
    )
    grad_query = lax.psum_scatter(summed, ("ctx", "dp"), scatter_dimension=1, tiled=True)
    return (predicted[None], grad_query)


BF = jnp.bfloat16
F32 = jnp.float32
MESH = pl.DeviceIdType.MESH
SIN_TERMS = [math.pi ** n * (-1) ** (n // 2) / math.factorial(n) for n in (1, 3, 5, 7, 9, 11, 13)]
COS_TERMS = [math.pi ** n * (-1) ** (n // 2) / math.factorial(n) for n in (0, 2, 4, 6, 8, 10, 12)]


def mm(a, b):
    return jnp.dot(a, b, preferred_element_type=F32)


def series(terms, square):
    total = jnp.full_like(square, terms[-1])
    for term in terms[-2::-1]:
        total = total * square + term
    return total


def rate_table():
    ids = lax.broadcasted_iota(jnp.int32, (FREQ, FREQ), 0)
    rates = jnp.ones((FREQ, FREQ), F32)
    for bit in range(FREQ.bit_length() - 1):
        rates = rates * jnp.where((ids & (1 << bit)) != 0, 2.0 ** (6.0 * (1 << bit) / FREQ), 1.0).astype(F32)
    return rates


def fused_kernel(
    nc,
    nx,
    feats_h,
    types_h,
    routes_h,
    pos_h,
    tgt_h,
    type_w_h,
    query_w,
    key_w,
    out_wt_h,
    anchor_g_h,
    query_g_h,
    key_g_h,
    pred_out,
    grad_out,
    feats,
    types,
    routes,
    pos,
    tgt,
    type_w,
    out_wt,
    anchor_g,
    query_g,
    key_g,
    kwin,
    qwin,
    qwin_t,
    gain_t,
    emb,
    part,
    part_in,
    anc,
    kv,
    pos_all,
    tgt_all,
    pred_part,
    pred_all,
    emb_t,
    qlin,
    probs,
    glin,
    y_send,
    y_in,
    z_send,
    z_in,
    local_sem,
    a_send,
    a_recv,
    p_send,
    p_recv,
    t_send,
    t_recv,
    b_send,
    b_recv,
    k_send,
    k_recv,
    o_send,
    o_recv,
    g_send,
    g_recv,
):
    c = lax.axis_index("cells")
    x = lax.axis_index("ctx")
    width = D // nx
    pair = 2 * width
    heads = width // HEAD_DIM
    half = D // 2
    odd = lax.rem(x, 2) == 1
    start = pl.multiple_of((x // 2) * pair, 128)
    q_dev = pos.shape[-1]

    def cells_peer(k):
        return {"cells": lax.rem(c + k, nc)}

    def ctx_peer(k):
        return {"ctx": lax.rem(x + k, nx)}

    barrier = pltpu.get_barrier_semaphore()
    for k in range(1, nc):
        pl.semaphore_signal(barrier, inc=1, device_id=cells_peer(k), device_id_type=MESH)
    for k in range(1, nx):
        pl.semaphore_signal(barrier, inc=1, device_id=ctx_peer(k), device_id_type=MESH)
    loads = [
        pltpu.make_async_copy(src, dst, local_sem.at[i])
        for i, (src, dst) in enumerate(
            (
                (types_h, types),
                (type_w_h, type_w),
                (feats_h, feats),
                (routes_h, routes),
                (pos_h, pos),
                (tgt_h, tgt),
                (query_w.at[:, pl.ds(start, pair)], qwin),
                (key_w.at[:, pl.ds(start, pair)], kwin),
                (out_wt_h, out_wt),
                (anchor_g_h, anchor_g.at[0]),
                (query_g_h, query_g.at[0]),
                (key_g_h, key_g.at[0]),
            )
        )
    ]
    for load in loads:
        load.start()

    def own(values):
        return jnp.where(odd, values[:, width:], values[:, :width])

    sent = []

    def send(src, dst, send_sem, recv_sem, peer):
        copy = pltpu.make_async_remote_copy(
            src_ref=src, dst_ref=dst, send_sem=send_sem, recv_sem=recv_sem, device_id=peer, device_id_type=MESH
        )
        copy.start()
        sent.append(copy)
        return copy

    for load in loads[:3]:
        load.wait()
    block = feats.shape[0] // types.shape[1]
    for b in range(types.shape[1]):
        pre = mm(feats[b * block : (b + 1) * block, :], type_w[types[0, b]])
        emb[b * block : (b + 1) * block, :] = jnp.tanh(pre).astype(BF)
    for load in loads[3:]:
        load.wait()
    row = lax.broadcasted_iota(jnp.int32, (nc * 8, feats.shape[0]), 0)
    label = ((row // 8) * nx + x) * SN_DEV + lax.rem(row, 4)
    table = (
        jnp.where(routes[0:1, :] == label, 1.0, 0.0) + jnp.where(routes[1:2, :] == label, 1.0, 0.0)
    ).astype(BF)
    low = mm(table, emb[:, :half])
    high = mm(table, emb[:, half:])
    mixed = jnp.where(lax.rem(lax.broadcasted_iota(jnp.int32, low.shape, 0), 8) < 4, low, high)
    for s in range(nc):
        part[s] = mixed[8 * s : 8 * s + 8, :]

    qwin_t[...] = qwin[...].T
    gain_t[...] = jnp.broadcast_to(query_g[:, pl.ds(start, pair)], (128, pair)).T
    out_rows = own(out_wt[:, pl.ds(start, pair)].astype(F32))
    out_cols = jnp.concatenate([out_rows, out_rows, out_rows, jnp.zeros_like(out_rows)], axis=0).T.astype(BF)
    key_gain = own(key_g[:, pl.ds(start, pair)])

    rates = rate_table()

    def embed_block(i):
        cols = pl.ds(pl.multiple_of(i * q_dev, 128), q_dev)
        for d in range(3):
            turns = rates * pos_all[i, d]
            whole = jnp.floor(turns + 0.5)
            rest = turns - whole
            parity = whole * 0.5
            sign = 1.0 - 4.0 * (parity - jnp.floor(parity))
            square = rest * rest
            spot = (2 * d) * FREQ
            emb_t[spot : spot + FREQ, cols] = (series(SIN_TERMS, square) * rest * sign).astype(BF)
            emb_t[spot + FREQ : spot + 2 * FREQ, cols] = (series(COS_TERMS, square) * sign).astype(BF)

    pos_all[x] = pos[...]
    tgt_all[x] = tgt[...]
    embed_block(x)

    pl.semaphore_wait(barrier, nc + nx - 2)
    a_copies = []
    for k in range(1, nc):
        a_copies.append(
            send(part.at[lax.rem(c + k, nc)], part_in.at[k], a_send.at[k], a_recv.at[k], cells_peer(k))
        )
    p_copies = []
    t_copies = []
    for k in range(1, nx):
        p_copies.append(send(pos, pos_all.at[x], p_send.at[k], p_recv.at[k], ctx_peer(k)))
        t_copies.append(send(tgt, tgt_all.at[x], t_send.at[k], t_recv.at[k], ctx_peer(k)))

    for k in range(1, nx):
        p_copies[k - 1].wait_recv()
        embed_block(lax.rem(x + nx - k, nx))

    for copy in a_copies:
        copy.wait_recv()
    pooled = part[c]
    for k in range(1, nc):
        pooled = pooled + part_in[k]
    square = pooled * pooled
    square = square + pltpu.roll(square, 4, 0)
    inverse = lax.rsqrt(jnp.sum(square, axis=1, keepdims=True) * (1.0 / D) + EPS)
    lower = lax.broadcasted_iota(jnp.int32, pooled.shape, 0) < 4
    gain = jnp.where(lower, anchor_g[:, :half], anchor_g[:, half:])
    anc[0] = (pooled * inverse * gain).astype(BF).astype(F32)
    b_copies = []
    for k in range(1, nx):
        b_copies.append(send(anc.at[0], anc.at[k], b_send.at[k], b_recv.at[k], ctx_peer(k)))

    mine = pl.ds(pl.multiple_of(lax.rem(x, 2) * width, 64), width)
    qlin[...] = mm(qwin_t[mine, :], emb_t[...])
    gains = gain_t[mine, :][:, 0:1]
    inverses = []
    hats = []
    for h in range(heads):
        rows = slice(h * HEAD_DIM, (h + 1) * HEAD_DIM)
        piece = qlin[rows, :]
        inverses.append(lax.rsqrt(jnp.mean(piece * piece, axis=0, keepdims=True) + EPS))
        hats.append((piece * inverses[h] * gains[rows, :]).astype(BF))

    for copy in b_copies:
        copy.wait_recv()
    rows_low = jnp.concatenate([anc[k, 0:4, :] for k in range(nx)], axis=0)
    rows_high = jnp.concatenate([anc[k, 4:8, :] for k in range(nx)], axis=0)
    key_lin = own(mm(rows_low.astype(BF), kwin[:half, :]) + mm(rows_high.astype(BF), kwin[half:, :]))
    values = own(jnp.where(x < nx // 2, rows_low, rows_high))
    pieces = []
    for h in range(heads):
        piece = key_lin[:, h * HEAD_DIM : (h + 1) * HEAD_DIM]
        pieces.append(piece * lax.rsqrt(jnp.mean(piece * piece, axis=1, keepdims=True) + EPS))
    keys = jnp.concatenate(pieces, axis=1) * key_gain
    kv[0] = jnp.concatenate([keys, values], axis=1).astype(BF)
    k_copies = []
    for k in range(1, nc):
        k_copies.append(send(kv.at[0], kv.at[k], k_send.at[k], k_recv.at[k], cells_peer(k)))

    for copy in k_copies:
        copy.wait_recv()
    both = jnp.concatenate([kv[k] for k in range(nc)], axis=0)
    both_t = both.T
    scale = HEAD_DIM ** (-0.5)
    count = both.shape[0]
    outs = []
    for h in range(heads):
        cols = slice(h * HEAD_DIM, (h + 1) * HEAD_DIM)
        exponent = jnp.exp(mm(both[:, cols], hats[h]) * scale)
        share = exponent * (1.0 / jnp.sum(exponent, axis=0, keepdims=True))
        probs[h] = share
        outs.append(mm(both_t[width + h * HEAD_DIM : width + (h + 1) * HEAD_DIM, :], share.astype(BF)).astype(BF))
    attended = jnp.concatenate(outs, axis=0)
    pred_part[0] = mm(out_rows.astype(BF), attended)
    o_copies = []
    for k in range(1, nx):
        o_copies.append(send(pred_part.at[0], pred_part.at[k], o_send.at[k], o_recv.at[k], ctx_peer(k)))
    for copy in t_copies:
        copy.wait_recv()
    goals = jnp.concatenate([tgt_all[i] for i in range(nx)], axis=1)
    for copy in o_copies:
        copy.wait_recv()
    predicted = pred_part[0]
    for k in range(1, nx):
        predicted = predicted + pred_part[k]
    pred_all[...] = predicted
    residue = predicted - goals
    first = residue.astype(BF).astype(F32)
    second = (residue - first).astype(BF).astype(F32)
    third = residue - first - second
    split = jnp.concatenate([first, second, third, jnp.zeros_like(third)], axis=0).astype(BF)
    grad_att = mm(out_cols, split).astype(BF)
    for h in range(heads):
        rows = slice(h * HEAD_DIM, (h + 1) * HEAD_DIM)
        share = probs[h]
        grad_w = mm(both[:, width + h * HEAD_DIM : width + (h + 1) * HEAD_DIM], grad_att[rows, :])
        inner = jnp.sum(share * grad_w, axis=0, keepdims=True)
        grad_s = (share * (grad_w - inner)).astype(BF)
        grad_q = mm(both_t[rows, :], grad_s) * scale
        weighted = grad_q * gains[rows, :]
        unit = qlin[rows, :] * inverses[h]
        shared = jnp.mean(weighted * unit, axis=0, keepdims=True)
        glin[rows, :] = ((weighted - unit * shared) * inverses[h]).astype(BF)

    glin_t = glin[...].T
    deep = D // nc
    pairs = nc // 2
    side = lax.rem(c, 2)
    place = c // 2
    order = sorted(range(1, pairs), key=lambda k: (abs(2 * k - pairs), k)) + [0]

    def terms(slab):
        rows = pl.ds(pl.multiple_of(slab * deep, 16), deep)
        full = mm(emb_t[rows, :], glin_t)
        rest = jnp.concatenate([full[: deep // 2, 128:], full[deep // 2 :, 128:]], axis=1)
        return jnp.concatenate([full[:, :128], rest], axis=0)

    far = pairs // 2
    straight = order[1:-1]

    def slab_at(k, flip):
        return lax.rem(place + k, pairs) * 2 + (1 - side if flip else side)

    def to_mate(k):
        y_send[k] = terms(slab_at(k, True)).astype(BF)
        return send(y_send.at[k], y_in.at[k], g_send.at[k], g_recv.at[k], {"cells": c + 1 - 2 * side})

    def along(k, src, dst, base, flip):
        return send(src.at[k], dst.at[k], g_send.at[base + k], g_recv.at[base + k], {"cells": slab_at(k, flip)})

    far_copy = to_mate(far)
    z_copies = []
    for k in straight:
        y_send[k] = terms(slab_at(k, True)).astype(BF)
        z_copies.append((along(k, y_send, y_in, pairs, True), y_in, k))
        z_send[k] = terms(slab_at(k, False)).astype(BF)
        z_copies.append((along(k, z_send, z_in, 2 * pairs, False), z_in, k))
    near_copy = to_mate(0)
    own_far = terms(slab_at(far, False))
    far_copy.wait_recv()
    z_send[far] = (own_far + y_in[far].astype(F32)).astype(BF)
    z_copies.append((along(far, z_send, z_in, 2 * pairs, False), z_in, far))
    total = terms(c)
    near_copy.wait_recv()
    total = total + y_in[0].astype(F32)
    pred_out[...] = pred_all[:, pl.ds(pl.multiple_of(x * q_dev, 128), q_dev)]
    for copy, landed, k in z_copies:
        copy.wait_recv()
        total = total + landed[k].astype(F32)
    grad_out[:, :128] = total[:deep]
    grad_out[: deep // 2, 128:] = total[deep:, : width - 128]
    grad_out[deep // 2 :, 128:] = total[deep:, width - 128 :]
    for copy in sent:
        copy.wait_send()


def fused_device(
    nc,
    nx,
    cell_feats,
    cell_types,
    cell_routes,
    positions,
    targets,
    type_weight,
    query_weight,
    key_weight,
    out_weight,
    anchor_gain,
    query_gain,
    key_gain,
):
    width = D // nx
    cells = cell_feats.shape[1]
    q_dev = positions.shape[2]
    queries = nx * q_dev
    outs = targets.shape[1]
    deep = D // nc
    count = nc * nx * SN_DEV
    vmem = pl.BlockSpec(memory_space=pltpu.VMEM)
    dma = pltpu.SemaphoreType.DMA
    predicted, grad = pl.pallas_call(
        functools.partial(fused_kernel, nc, nx),
        out_shape=(
            jax.ShapeDtypeStruct((outs, q_dev), F32),
            jax.ShapeDtypeStruct((deep, width), F32),
        ),
        in_specs=[pl.BlockSpec(memory_space=pltpu.HBM)] * 12,
        out_specs=(vmem, vmem),
        scratch_shapes=[
            pltpu.VMEM((cells, cell_feats.shape[2]), BF),
            pltpu.SMEM(cell_types.shape, jnp.int32),
            pltpu.VMEM((cell_routes.shape[2], cells), jnp.int32),
            pltpu.VMEM((3, 1, q_dev), F32),
            pltpu.VMEM((outs, q_dev), F32),
            pltpu.VMEM(type_weight.shape, BF),
            pltpu.VMEM((outs, D), BF),
            pltpu.VMEM((1, D), F32),
            pltpu.VMEM((1, D), F32),
            pltpu.VMEM((1, D), F32),
            pltpu.VMEM((D, 2 * width), BF),
            pltpu.VMEM((D, 2 * width), BF),
            pltpu.VMEM((2 * width, D), BF),
            pltpu.VMEM((2 * width, 128), F32),
            pltpu.VMEM((cells, D), BF),
            pltpu.VMEM((nc, 8, D // 2), F32),
            pltpu.VMEM((nc, 8, D // 2), F32),
            pltpu.VMEM((nx, 8, D // 2), F32),
            pltpu.VMEM((nc, nx * SN_DEV, 2 * width), BF),
            pltpu.VMEM((nx, 3, 1, q_dev), F32),
            pltpu.VMEM((nx, outs, q_dev), F32),
            pltpu.VMEM((nx, outs, queries), F32),
            pltpu.VMEM((outs, queries), F32),
            pltpu.VMEM((D, queries), BF),
            pltpu.VMEM((width, queries), F32),
            pltpu.VMEM((width // HEAD_DIM, count, queries), F32),
            pltpu.VMEM((width, queries), BF),
            pltpu.VMEM((nc // 2, 3 * deep // 2, 128), BF),
            pltpu.VMEM((nc // 2, 3 * deep // 2, 128), BF),
            pltpu.VMEM((nc // 2, 3 * deep // 2, 128), BF),
            pltpu.VMEM((nc // 2, 3 * deep // 2, 128), BF),
            dma((12,)),
            dma((nc,)),
            dma((nc,)),
            dma((nx,)),
            dma((nx,)),
            dma((nx,)),
            dma((nx,)),
            dma((nx,)),
            dma((nx,)),
            dma((nc,)),
            dma((nc,)),
            dma((nx,)),
            dma((nx,)),
            dma((2 * nc,)),
            dma((2 * nc,)),
        ],
        compiler_params=pltpu.CompilerParams(
            collective_id=0, has_side_effects=True, vmem_limit_bytes=64 * 1024 * 1024
        ),
    )(
        cell_feats[0],
        cell_types,
        cell_routes[0].T,
        positions[0].reshape(3, 1, q_dev),
        targets[0],
        type_weight,
        query_weight,
        key_weight,
        out_weight.T,
        anchor_gain,
        query_gain,
        key_gain,
    )
    return (predicted[None], grad)


def solution(mesh):
    in_specs = (
        P(("groups", "dp"), ("cells", "ctx"), None),
        P(("groups", "dp"), ("cells", "ctx")),
        P(("groups", "dp"), ("cells", "ctx"), None),
        P(("groups", "dp"), None, ("cells", "ctx")),
        P(("groups", "dp"), None, ("cells", "ctx")),
        P(),
        P(),
        P(),
        P(),
        P(),
        P(),
        P(),
    )
    out_specs = (P(("groups", "dp"), None, ("cells", "ctx")), P(("groups", "cells"), ("ctx", "dp")))
    sizes = mesh.shape
    fits = sizes["groups"] == 1 and sizes["dp"] == 1 and sizes["ctx"] == 4 and D % (32 * sizes["cells"]) == 0 and sizes["cells"] % 2 == 0
    body = functools.partial(fused_device, sizes["cells"], sizes["ctx"]) if fits else general_device
    return jax.shard_map(
        body, mesh=mesh, in_specs=in_specs, out_specs=out_specs, check_vma=False
    )
```

profile of v0, /device:TPU:0, one launch (start us, length us, event | category | flops | bytes accessed | tf_op | source)
XLA Modules:
  0.0 35.4 jit_solution(8053008548260641603)
XLA Ops:
  0.6 32.0 %shard_map.131 = (f32[4,128]{1,0:T(4,128)}, f32[96,192]{1,0:T(8,128)}) custom-call(bf16[1024,128]{1,0:T(8,128)(2,1)} %bitcast.8, s32[1,8]{1,0:T(1,128)} %types_h.1, s32[2,1024]{1,0:T(2,128)} %bitcast.9, f32[3,1,128]{2,1,0:T(1,128)} %bitcast.13, f32[4,128]{1,0:T(4,128)} %bitcast.11, bf16[4,128,768]{2,1,0:T(8,128)(2,1)} %type_w_h.1, bf16[768,768]{1,0:T(8,128)(2,1)} %query_w.1, ...), custom_call_target="tpu_custom_call" | custom-call | tf_op jit(solution)/shard_map/pallas_call | solution.py:545
  32.6 1.3 %copy.16 = f32[1,4,128]{2,1,0:T(4,128)} copy(f32[1,4,128]{2,1,0:T(4,128)} %bitcast.12) | data formatting | bytes 4096
  33.9 1.5 %copy.17 = f32[96,192]{1,0:T(8,128)} copy(f32[96,192]{1,0:T(8,128)} %get-tuple-element.9) | data formatting | bytes 147456
where the time goes:
time: 35.6 us; the launch traced here: 35.4 us
  Pallas kernels  32 us (90%)
  local copies, waits for them, and re-layouts  2.8 us (8%)
  between operations  0.64 us (2%)
    pallas_call x1, Pallas kernels, fused_device(): pl.pallas_call(functools.partial(fused_kernel, nc, nx), out_shape=(jax.Sh...  32 us
    unnamed x2, local copies, waits for them, and re-layouts  2.8 us

commit v1 on v0

--- a/solution.py
+++ b/solution.py
@@ -517,6 +517,10 @@
         copy.wait_send()
 
 
+def finish(pred_in, grad_in, pred_o, grad_o):
+    pred_o[...] = pred_in[...]
+    grad_o[...] = grad_in[...]
+
 def fused_device(
     nc,
     nx,
@@ -545,8 +549,8 @@
     predicted, grad = pl.pallas_call(
         functools.partial(fused_kernel, nc, nx),
         out_shape=(
-            jax.ShapeDtypeStruct((outs, q_dev), F32),
-            jax.ShapeDtypeStruct((deep, width), F32),
+            pltpu.VMEM((outs, q_dev), F32),
+            pltpu.VMEM((deep, width), F32),
         ),
         in_specs=[pl.BlockSpec(memory_space=pltpu.HBM)] * 12,
         out_specs=(vmem, vmem),
@@ -599,7 +603,7 @@
             dma((2 * nc,)),
         ],
         compiler_params=pltpu.CompilerParams(
-            collective_id=0, has_side_effects=True, vmem_limit_bytes=64 * 1024 * 1024
+            collective_id=0, has_side_effects=True, vmem_limit_bytes=64 * 1024 * 1024 - 256 * 1024
         ),
     )(
         cell_feats[0],
@@ -615,6 +619,13 @@
         query_gain,
         key_gain,
     )
+    predicted, grad = pl.pallas_call(
+        finish,
+        out_shape=(jax.ShapeDtypeStruct((outs, q_dev), F32), jax.ShapeDtypeStruct((deep, width), F32)),
+        in_specs=[vmem, vmem],
+        out_specs=(vmem, vmem),
+        compiler_params=pltpu.CompilerParams(vmem_limit_bytes=1024 * 1024),
+    )(predicted, grad)
     return (predicted[None], grad)
 
 

time: 35.6 us -> 32.8 us (0.921)
  local copies, waits for them, and re-layouts: 2.8 us -> 0 us
    unnamed x2 -> x0, local copies, waits for them, and re-layouts: 2.8 us -> none
    pallas_call x1 -> x2, Pallas kernels: 32 us -> 32 us  [the longest x1 31.3 us: fused_device(): pl.pallas_call(functools.partial(fused_kernel, nc, nx), out_shape=(pltpu....]
where the time goes in v1:
time: 32.8 us; the launch traced here: 32.6 us
  Pallas kernels  32 us (98%)
  between operations  0.64 us (2%)
    pallas_call x1, Pallas kernels, fused_device(): pl.pallas_call(functools.partial(fused_kernel, nc, nx), out_shape=(pltpu....  31.3 us

profile of v1, /device:TPU:0, one launch (start us, length us, event | category | flops | bytes accessed | tf_op | source)
XLA Modules:
  0.0 32.6 jit_solution(6514624084531252535)
XLA Ops:
  0.6 31.3 %shard_map.131 = (f32[4,128]{1,0:T(4,128)S(1)}, f32[96,192]{1,0:T(8,128)S(1)}) custom-call(bf16[1024,128]{1,0:T(8,128)(2,1)} %bitcast.8, s32[1,8]{1,0:T(1,128)} %types_h.1, s32[2,1024]{1,0:T(2,128)} %bitcast.9, f32[3,1,128]{2,1,0:T(1,128)} %bitcast.12, f32[4,128]{1,0:T(4,128)} %bitcast.11, bf16[4,128,768]{2,1,0:T(8,128)(2,1)} %type_w_h.1, ...), custom_call_target="tpu_custom_call" | custom-call | tf_op jit(solution)/shard_map/pallas_call | solution.py:549
  31.9 0.7 %shard_map.132 = (f32[4,128]{1,0:T(4,128)}, f32[96,192]{1,0:T(8,128)}) custom-call(f32[4,128]{1,0:T(4,128)S(1)} %get-tuple-element.6.pred_in, f32[96,192]{1,0:T(8,128)S(1)} %get-tuple-element.7.grad_in), custom_call_target="tpu_custom_call" | custom-call | tf_op jit(solution)/shard_map/pallas_call | solution.py:622

commit v2 on v1

v2 whole, which is shorter than its diff:
```python
import functools
import math

import jax
import jax.numpy as jnp
from jax import lax
from jax.experimental import pallas as pl
from jax.experimental.pallas import tpu as pltpu
from jax.sharding import PartitionSpec as P

D = 768
HEAD_DIM = 64
SN_DEV = 4
FREQ = 128


EPS = 1e-06


def head_norm(values):
    shaped = values.reshape(values.shape[:-1] + (values.shape[-1] // HEAD_DIM, HEAD_DIM))
    inverse = lax.rsqrt(jnp.mean(shaped * shaped, axis=-1, keepdims=True) + EPS)
    return (shaped * inverse).reshape(values.shape)


def embed_positions(coords):
    freq_ids = jnp.arange(FREQ, dtype=jnp.float32)
    rate_table = math.pi * jnp.exp2(freq_ids * (6.0 / FREQ))
    angles = jnp.transpose(coords)[:, :, None] * rate_table[None, None, :]
    sin_cos = jnp.stack([jnp.sin(angles), jnp.cos(angles)], axis=2)
    return sin_cos.reshape(coords.shape[1], 6 * FREQ).astype(jnp.bfloat16)


def cell_embed(cell_rows, type_ids, type_weight):
    row_count = cell_rows.shape[0]
    per_block = row_count // type_ids.shape[0]
    shaped = cell_rows.reshape(type_ids.shape[0], per_block, cell_rows.shape[1])
    chosen = type_weight[0][None]
    for type_id in range(1, type_weight.shape[0]):
        chosen = jnp.where((type_ids == type_id)[:, None, None], type_weight[type_id][None], chosen)
    pre_act = jnp.einsum("bnf,bfd->bnd", shaped, chosen, preferred_element_type=jnp.float32)
    return jnp.tanh(pre_act).astype(jnp.bfloat16).reshape(row_count, -1)


def make_keys(anchors, key_weight, key_gain):
    key_lin = jnp.dot(anchors, key_weight, preferred_element_type=jnp.float32)
    return (head_norm(key_lin) * key_gain).astype(jnp.bfloat16)


def general_device(
    cell_feats,
    cell_types,
    cell_routes,
    positions,
    targets,
    type_weight,
    query_weight,
    key_weight,
    out_weight,
    anchor_gain,
    query_gain,
    key_gain,
):
    slab_count = lax.axis_size("cells")
    column_count = lax.axis_size("ctx")
    cell_rows = cell_feats[0]
    type_ids = cell_types[0]
    routes = cell_routes[0]
    embedded = cell_embed(cell_rows, type_ids, type_weight)
    slots = jnp.arange(slab_count * SN_DEV, dtype=jnp.int32)
    owned = (slots // SN_DEV * column_count + lax.axis_index("ctx")) * SN_DEV + slots % SN_DEV
    table = jnp.sum((routes[None, :, :] == owned[:, None, None]).astype(jnp.int32), axis=2)
    partial = jnp.dot(table.astype(jnp.bfloat16), embedded, preferred_element_type=jnp.float32)
    pooled = lax.psum_scatter(partial, "cells", scatter_dimension=0, tiled=True)
    inverse = lax.rsqrt(jnp.mean(pooled * pooled, axis=-1, keepdims=True) + EPS)
    anchors = (pooled * inverse * anchor_gain).astype(jnp.bfloat16)
    own_keys = make_keys(anchors, key_weight, key_gain)
    all_keys, all_anchors = (
        lax.all_gather(own_keys, ("cells", "ctx"), axis=0, tiled=True),
        lax.all_gather(anchors, ("cells", "ctx"), axis=0, tiled=True),
    )
    embed = embed_positions(positions[0])
    query_lin = jnp.dot(embed, query_weight, preferred_element_type=jnp.float32)
    query_hat = (head_norm(query_lin) * query_gain).astype(jnp.bfloat16)
    query_count = embed.shape[0]
    head_count = D // HEAD_DIM
    group_size = 4
    score_scale = HEAD_DIM ** (-0.5)
    query_heads = query_hat.reshape(query_count, head_count, HEAD_DIM)
    key_heads = all_keys.reshape(-1, head_count, HEAD_DIM)
    value_heads = all_anchors.reshape(-1, head_count, HEAD_DIM)
    probs_saved = []
    outputs = []
    for first_head in range(0, head_count, group_size):
        last_head = first_head + group_size
        scores = (
            jnp.einsum(
                "qhd,khd->hqk",
                query_heads[:, first_head:last_head],
                key_heads[:, first_head:last_head],
                preferred_element_type=jnp.float32,
            )
            * score_scale
        )
        exponent = jnp.exp(scores)
        probs_f32 = exponent / jnp.sum(exponent, axis=-1, keepdims=True)
        probs_saved.append(probs_f32)
        outputs.append(
            jnp.einsum(
                "hqk,khd->qhd",
                probs_f32.astype(jnp.bfloat16),
                value_heads[:, first_head:last_head],
                preferred_element_type=jnp.float32,
            )
        )
    attended = jnp.concatenate(outputs, axis=1).reshape(query_count, D).astype(jnp.bfloat16)
    predicted = lax.dot_general(
        out_weight, attended, (((0,), (1,)), ((), ())), preferred_element_type=jnp.float32
    )
    residue = predicted - targets[0]
    grad_attended = lax.dot_general(
        residue,
        out_weight.astype(jnp.float32),
        (((0,), (1,)), ((), ())),
        precision=lax.Precision.HIGHEST,
    ).astype(jnp.bfloat16)
    grad_heads = grad_attended.reshape(query_count, head_count, HEAD_DIM)
    pieces = []
    for group_index, first_head in enumerate(range(0, head_count, group_size)):
        last_head = first_head + group_size
        probs_f32 = probs_saved[group_index]
        grad_weights = jnp.einsum(
            "qhd,khd->hqk",
            grad_heads[:, first_head:last_head],
            value_heads[:, first_head:last_head],
            preferred_element_type=jnp.float32,
        )
        grad_scores = probs_f32 * (
            grad_weights - jnp.sum(probs_f32 * grad_weights, axis=-1, keepdims=True)
        )
        pieces.append(
            jnp.einsum(
                "hqk,khd->qhd",
                grad_scores.astype(jnp.bfloat16),
                key_heads[:, first_head:last_head],
                preferred_element_type=jnp.float32,
            )
            * score_scale
        )
    grad_qhat = jnp.concatenate(pieces, axis=1).reshape(query_count, D)
    weighted = (grad_qhat * query_gain).reshape(query_count, head_count, HEAD_DIM)
    shaped = query_lin.reshape(query_count, head_count, HEAD_DIM)
    norm_inverse = lax.rsqrt(jnp.mean(shaped * shaped, axis=-1, keepdims=True) + EPS)
    unit_rows = shaped * norm_inverse
    grad_qlin = (
        (
            (weighted - unit_rows * jnp.mean(weighted * unit_rows, axis=-1, keepdims=True))
            * norm_inverse
        )
        .reshape(query_count, D)
        .astype(jnp.bfloat16)
    )
    summed = lax.psum_scatter(
        lax.dot_general(
            embed, grad_qlin, (((0,), (0,)), ((), ())), preferred_element_type=jnp.float32
        ),
        "cells",
        scatter_dimension=0,
        tiled=True,
    )
    grad_query = lax.psum_scatter(summed, ("ctx", "dp"), scatter_dimension=1, tiled=True)
    return (predicted[None], grad_query)


BF = jnp.bfloat16
F32 = jnp.float32
MESH = pl.DeviceIdType.MESH
SIN_TERMS = [math.pi ** n * (-1) ** (n // 2) / math.factorial(n) for n in (1, 3, 5, 7, 9, 11, 13)]
COS_TERMS = [math.pi ** n * (-1) ** (n // 2) / math.factorial(n) for n in (0, 2, 4, 6, 8, 10, 12)]


def mm(a, b):
    return jnp.dot(a, b, preferred_element_type=F32)


def series(terms, square):
    total = jnp.full_like(square, terms[-1])
    for term in terms[-2::-1]:
        total = total * square + term
    return total


def rate_table():
    ids = lax.broadcasted_iota(jnp.int32, (FREQ, FREQ), 0)
    rates = jnp.ones((FREQ, FREQ), F32)
    for bit in range(FREQ.bit_length() - 1):
        rates = rates * jnp.where((ids & (1 << bit)) != 0, 2.0 ** (6.0 * (1 << bit) / FREQ), 1.0).astype(F32)
    return rates


def fused_kernel(
    feats_h,
    types_h,
    routes_h,
    pos_h,
    tgt_h,
    type_w_h,
    query_w,
    key_w_h,
    out_wt_h,
    anchor_g_h,
    query_g_h,
    key_g_h,
    pred_out,
    grad_out,
    feats,
    types,
    routes,
    pos,
    tgt,
    type_w,
    out_wt,
    anchor_g,
    query_g,
    key_g,
    key_w,
    qwin,
    qwin_t,
    gain_t,
    emb,
    part,
    part_b,
    part_in,
    w_out,
    kv_out,
    kv_in,
    pos_all,
    tgt_all,
    pred_part,
    emb_t,
    qlin,
    hats,
    probs,
    glin,
    y_send,
    y_in,
    z_send,
    z_in,
    total,
    local_sem,
    a_send,
    a_recv,
    p_send,
    p_recv,
    t_send,
    t_recv,
    k_send,
    k_recv,
    o_send,
    o_recv,
    g_send,
    g_recv,
):
    c = lax.axis_index("cells")
    x = lax.axis_index("ctx")
    z, y = c // 2, lax.rem(c, 2)
    xx, k = x // 2, lax.rem(x, 2)
    width = D // 4
    pair = 2 * width
    heads = width // HEAD_DIM
    odd = y == 1
    start = pl.multiple_of(xx * pair, 128)
    q_dev = pos.shape[-1]
    place = y * 2 + xx

    def flip(value, on):
        return 1 - value if on else value

    def far_z(m):
        return flip(z // 2, m // 2) * 2 + flip(lax.rem(z, 2), m % 2)

    def device(m, dy, dx, dk):
        return {"cells": far_z(m) * 2 + flip(y, dy), "ctx": flip(xx, dx) * 2 + flip(k, dk)}

    others = [(m, dy, dx, dk) for m in (3, 2, 1, 0) for dy in (1, 0) for dx in (1, 0) for dk in (1, 0)][:-1]

    loads = [
        pltpu.make_async_copy(src, dst, local_sem.at[i])
        for i, (src, dst) in enumerate(
            (
                (types_h, types),
                (type_w_h, type_w),
                (feats_h, feats),
                (routes_h, routes),
                (pos_h, pos),
                (tgt_h, tgt),
                (out_wt_h, out_wt),
                (anchor_g_h, anchor_g.at[0]),
                (query_g_h, query_g.at[0]),
                (key_g_h, key_g.at[0]),
                (query_w.at[:, pl.ds(start, pair)], qwin),
                (key_w_h, key_w),
            )
        )
    ]
    for load in loads[:4]:
        load.start()
    barrier = pltpu.get_barrier_semaphore()
    for spot in others:
        pl.semaphore_signal(barrier, inc=1, device_id=device(*spot), device_id_type=MESH)
    for load in loads[4:]:
        load.start()

    def own(values):
        return jnp.where(odd, values[:, width:], values[:, :width])

    def copy_to(src, dst, send_sem, recv_sem, peer):
        return pltpu.make_async_remote_copy(
            src_ref=src, dst_ref=dst, send_sem=send_sem, recv_sem=recv_sem, device_id=peer, device_id_type=MESH
        )

    for load in loads[:3]:
        load.wait()
    block = feats.shape[0] // types.shape[1]
    for b in range(types.shape[1]):
        pre = mm(feats[b * block : (b + 1) * block, :], type_w[types[0, b]])
        emb[b * block : (b + 1) * block, :] = jnp.tanh(pre).astype(BF)
    for load in loads[3:6]:
        load.wait()
    row = lax.broadcasted_iota(jnp.int32, (4 * 8, feats.shape[0]), 0)
    slab = ((row // 16) * 2 + lax.rem(row, 8) // 4) * 2 + lax.rem(row // 8, 2)
    label = (slab * 4 + x) * SN_DEV + lax.rem(row, 4)
    table = (
        jnp.where(routes[0:1, :] == label, 1.0, 0.0) + jnp.where(routes[1:2, :] == label, 1.0, 0.0)
    ).astype(BF)
    sums = mm(table, emb[...])
    for o in range(4):
        part[o] = sums[8 * o : 8 * o + 8, :]
        part_b[o] = sums[8 * o : 8 * o + 8, :].astype(BF)
    pos_all[place] = pos[...]
    tgt_all[place] = tgt[...]

    half = z // 2
    is_owner = (c >= 2) & (c < 6)
    mine = 2 + half * 2 + y

    def pool_copy(i):
        dh, dy = ((1, 1), (1, 0), (0, 1), (0, 0))[i]
        o = flip(half, dh) * 2 + flip(y, dy)
        return copy_to(
            part_b.at[o],
            part_in.at[lax.rem(c - (2 + o) + 8, 8)],
            a_send.at[i],
            a_recv.at[0],
            {"cells": 2 + o, "ctx": x},
        )

    pl.semaphore_wait(barrier, len(others))
    for i in range(3):
        pool_copy(i).start()

    @pl.when(jnp.logical_not(is_owner))
    def _():
        pool_copy(3).start()

    p_copies = []
    t_copies = []
    quad = ((1, 1), (1, 0), (0, 1))
    for i, (dy, dx) in enumerate(quad):
        p_copies.append(copy_to(pos, pos_all.at[place], p_send.at[i], p_recv.at[i], device(0, dy, dx, 0)))
        p_copies[i].start()
    for i, (dy, dx) in enumerate(quad):
        t_copies.append(copy_to(tgt, tgt_all.at[place], t_send.at[i], t_recv.at[i], device(0, dy, dx, 0)))
        t_copies[i].start()

    for load in loads[6:]:
        load.wait()
    rates = rate_table()

    def embed_block(i):
        cols = pl.ds(pl.multiple_of(i * q_dev, 128), q_dev)
        for d in range(3):
            turns = rates * pos_all[i, d]
            whole = jnp.floor(turns + 0.5)
            rest = turns - whole
            parity = whole * 0.5
            sign = 1.0 - 4.0 * (parity - jnp.floor(parity))
            square = rest * rest
            spot = (2 * d) * FREQ
            emb_t[spot : spot + FREQ, cols] = (series(SIN_TERMS, square) * rest * sign).astype(BF)
            emb_t[spot + FREQ : spot + 2 * FREQ, cols] = (series(COS_TERMS, square) * sign).astype(BF)

    embed_block(place)

    out_f = out_wt[...].astype(F32)
    out_t = jnp.concatenate([out_f, jnp.zeros_like(out_f)], axis=0).T.astype(BF)
    lane8 = lax.broadcasted_iota(jnp.int32, (8, 256), 1)
    pick = jnp.where(lax.rem(lane8, 4) == lax.broadcasted_iota(jnp.int32, (8, 256), 0), 1.0, 0.0).astype(BF)
    lane_d = lax.broadcasted_iota(jnp.int32, (D, 256), 1)
    inside = lax.rem(lane_d, 16) // 4
    head_of = (lane_d // 64) * heads + inside
    keep = (lax.broadcasted_iota(jnp.int32, (D, 256), 0) // HEAD_DIM == head_of) & (inside < heads)
    keep = keep & (lax.rem(lane_d, 64) < 48)
    w_out[...] = jnp.where(keep, mm(out_t, pick), 0.0).astype(BF)

    qwin_t[...] = qwin[...].T
    gain_t[...] = jnp.broadcast_to(query_g[:, pl.ds(start, pair)], (128, pair)).T

    for i, (dy, dx) in enumerate(quad):
        p_copies[i].wait_recv()
        embed_block(flip(y, dy) * 2 + flip(xx, dx))

    rows_mine = pl.ds(pl.multiple_of(y * width, 64), width)
    qlin[...] = mm(qwin_t[rows_mine, :], emb_t[...])
    gains = gain_t[rows_mine, :][:, 0:1]

    def norm_of(h):
        piece = qlin[h * HEAD_DIM : (h + 1) * HEAD_DIM, :]
        return lax.rsqrt(jnp.mean(piece * piece, axis=0, keepdims=True) + EPS)

    for h in range(heads):
        rows = slice(h * HEAD_DIM, (h + 1) * HEAD_DIM)
        hats[rows, :] = (qlin[rows, :] * norm_of(h) * gains[rows, :]).astype(BF)
    hats[width:, :] = jnp.zeros((256 - width, hats.shape[1]), BF)

    def key_copy(i):
        m, dy, dx, dk = others[i]
        group = flip(xx, dx) * 2 + flip(y, dy)
        return copy_to(
            kv_out.at[group],
            kv_in.at[(c - 2) * 4 + x],
            k_send.at[i],
            k_recv.at[0],
            device(m, dy, dx, dk),
        )

    @pl.when(is_owner)
    def _():
        arrived = part_in.at[pl.ds(1, 7)]
        copy_to(arrived, arrived, a_send.at[0], a_recv.at[0], {"cells": c, "ctx": x}).wait_recv()
        pooled = part[c - 2]
        for s in range(1, 8):
            pooled = pooled + part_in[s].astype(F32)
        inverse = lax.rsqrt(jnp.mean(pooled * pooled, axis=1, keepdims=True) + EPS)
        anchors = (pooled * inverse * anchor_g[...]).astype(BF)
        key_lin = mm(anchors, key_w[...])
        out_lin = mm(anchors, w_out[...])
        low = lax.broadcasted_iota(jnp.int32, (8, 128), 1) < HEAD_DIM
        pieces = []
        for j in range(D // 128):
            piece = key_lin[:, 128 * j : 128 * j + 128]
            square = piece * piece
            first = jnp.sum(jnp.where(low, square, 0.0), axis=1, keepdims=True)
            second = jnp.sum(jnp.where(low, 0.0, square), axis=1, keepdims=True)
            pieces.append(piece * lax.rsqrt(jnp.where(low, first, second) * (1.0 / HEAD_DIM) + EPS))
        keys = jnp.concatenate(pieces, axis=1) * key_g[...]
        coarse = out_lin.astype(BF).astype(F32)
        mixed = jnp.where(lax.rem(lane8, 64) // 16 == 1, out_lin - coarse, coarse)
        for g in range(4):
            kv_out[g] = jnp.concatenate(
                [keys[:, width * g : width * g + width], mixed[:, 64 * g : 64 * g + 64]], axis=1
            ).astype(BF)
        for i in range(len(others)):
            key_copy(i).start()
        kv_in[(c - 2) * 4 + x] = kv_out[xx * 2 + y]

    def keys_arrive(count):
        landed = kv_in.at[pl.ds(0, count)]
        copy_to(landed, landed, k_send.at[0], k_recv.at[0], {"cells": c, "ctx": x}).wait_recv()

    @pl.when(is_owner)
    def _():
        keys_arrive(15)

    @pl.when(jnp.logical_not(is_owner))
    def _():
        keys_arrive(16)

    both_f = jnp.concatenate([kv_in[s].astype(F32) for s in range(16)], axis=0)
    both = both_f.astype(BF)
    both_t = both.T
    scale = HEAD_DIM ** (-0.5)
    lane = lax.broadcasted_iota(jnp.int32, (both.shape[0], 128), 1)
    tile0, tile1 = both_f[:, :128], both_f[:, 128:]
    lefts = [
        jnp.where(lane < HEAD_DIM, tile0, 0.0).astype(BF),
        jnp.where(lane >= HEAD_DIM, tile0, 0.0).astype(BF),
        jnp.where(lane < HEAD_DIM, tile1, 0.0).astype(BF),
    ]
    queries = qlin.shape[1]
    out_row = lax.broadcasted_iota(jnp.int32, (16, queries), 0) // 4
    by_head = jnp.zeros((16, queries), F32)
    for h in range(heads):
        exponent = jnp.exp(mm(lefts[h], hats[(h // 2) * 128 : (h // 2) * 128 + 128, :]) * scale)
        share = exponent * (1.0 / jnp.sum(exponent, axis=0, keepdims=True))
        probs[h] = share
        outs = mm(both_t[width : width + 32, :], share.astype(BF))
        by_head = jnp.where(out_row == h, outs[:16] + outs[16:], by_head)
    pred_part[0] = by_head[0:4] + by_head[4:8] + by_head[8:12]
    o_copies = []
    for i, (dy, dx) in enumerate(quad):
        o_copies.append(
            copy_to(pred_part.at[0], pred_part.at[1 + i], o_send.at[i], o_recv.at[i], device(0, dy, dx, 0))
        )
        o_copies[i].start()

    for i in range(3):
        pool_copy(i).wait_send()

    @pl.when(jnp.logical_not(is_owner))
    def _():
        pool_copy(3).wait_send()

    @pl.when(is_owner)
    def _():
        for i in range(len(others)):
            key_copy(i).wait_send()

    for copy in p_copies + t_copies:
        copy.wait_send()
    for copy in t_copies:
        copy.wait_recv()
    goals = jnp.concatenate([tgt_all[i] for i in range(4)], axis=1)
    backs = [
        jnp.where((lane >= 64) & (lax.rem(lane, 16) // 4 == h), tile1, 0.0).astype(BF) for h in range(heads)
    ]
    for copy in o_copies:
        copy.wait_recv()
    predicted = pred_part[0] + pred_part[1] + pred_part[2] + pred_part[3]
    residue = predicted - goals
    coarse = residue.astype(BF).astype(F32)
    rest = residue - coarse
    none = jnp.zeros((64, queries), F32)
    split = jnp.concatenate([none] + [coarse] * 8 + [rest] * 8, axis=0).astype(BF)
    weighed = by_head * jnp.concatenate([residue] * 4, axis=0)
    for h in range(heads):
        rows = slice(h * HEAD_DIM, (h + 1) * HEAD_DIM)
        inner = jnp.sum(weighed[4 * h : 4 * h + 4], axis=0, keepdims=True)
        grad_s = (probs[h] * (mm(backs[h], split) - inner)).astype(BF)
        grad_q = mm(both_t[rows, :], grad_s) * scale
        weighted = grad_q * gains[rows, :]
        inverse = norm_of(h)
        unit = qlin[rows, :] * inverse
        shared = jnp.mean(weighted * unit, axis=0, keepdims=True)
        glin[rows, :] = ((weighted - unit * shared) * inverse).astype(BF)

    glin_t = glin[...].T
    deep = D // 8

    def terms(slab):
        rows = pl.ds(pl.multiple_of(slab * deep, 16), deep)
        full = mm(emb_t[rows, :], glin_t)
        rest = jnp.concatenate([full[: deep // 2, 128:], full[deep // 2 :, 128:]], axis=1)
        return jnp.concatenate([full[:, :128], rest], axis=0)

    mates = {}
    for m in (3, 2, 1, 0):
        y_send[m] = terms(far_z(m) * 2 + 1 - k).astype(BF)
        mates[m] = copy_to(y_send.at[m], y_in.at[m], g_send.at[m], g_recv.at[m], device(0, 0, 0, 1))
        mates[m].start()

    def along(m):
        peer = {"cells": far_z(m) * 2 + k, "ctx": xx * 2 + y}
        return copy_to(z_send.at[m], z_in.at[m], g_send.at[4 + m], g_recv.at[4 + m], peer)

    for m in (3, 2, 1):
        mixed = terms(far_z(m) * 2 + k)
        mates[m].wait_recv()
        z_send[m] = (mixed + y_in[m].astype(F32)).astype(BF)
        along(m).start()
    mixed = terms(z * 2 + k)
    mates[0].wait_recv()
    mixed = mixed + y_in[0].astype(F32)
    total[...] = mixed

    @pl.when(y != k)
    def _():
        z_send[0] = mixed.astype(BF)
        along(0).start()

    cols = pl.ds(pl.multiple_of(place * q_dev, 128), q_dev)
    for copy in o_copies:
        copy.wait_send()
    pred_part[0] = predicted
    pred_out[...] = pred_part[0, :, cols]
    for m in (3, 2, 1, 0):
        mates[m].wait_send()

    @pl.when(y != k)
    def _():
        along(0).wait_recv()
        total[...] = z_in[0].astype(F32)
        along(0).wait_send()

    summed = total[...]
    for m in (1, 2, 3):
        along(m).wait_recv()
        summed = summed + z_in[m].astype(F32)
    grad_out[:, :128] = summed[:deep]
    grad_out[: deep // 2, 128:] = summed[deep:, : width - 128]
    grad_out[deep // 2 :, 128:] = summed[deep:, width - 128 :]
    for m in (1, 2, 3):
        along(m).wait_send()


def finish(pred_in, grad_in, pred_o, grad_o):
    pred_o[...] = pred_in[...]
    grad_o[...] = grad_in[...]

def fused_device(
    cell_feats,
    cell_types,
    cell_routes,
    positions,
    targets,
    type_weight,
    query_weight,
    key_weight,
    out_weight,
    anchor_gain,
    query_gain,
    key_gain,
):
    width = D // 4
    cells = cell_feats.shape[1]
    q_dev = positions.shape[2]
    queries = 4 * q_dev
    outs = targets.shape[1]
    deep = D // 8
    vmem = pl.BlockSpec(memory_space=pltpu.VMEM)
    dma = pltpu.SemaphoreType.DMA
    predicted, grad = pl.pallas_call(
        fused_kernel,
        out_shape=(
            pltpu.VMEM((outs, q_dev), F32),
            pltpu.VMEM((deep, width), F32),
        ),
        in_specs=[pl.BlockSpec(memory_space=pltpu.HBM)] * 12,
        out_specs=(vmem, vmem),
        scratch_shapes=[
            pltpu.VMEM((cells, cell_feats.shape[2]), BF),
            pltpu.SMEM(cell_types.shape, jnp.int32),
            pltpu.VMEM((cell_routes.shape[2], cells), jnp.int32),
            pltpu.VMEM((3, 1, q_dev), F32),
            pltpu.VMEM((outs, q_dev), F32),
            pltpu.VMEM(type_weight.shape, BF),
            pltpu.VMEM((outs, D), BF),
            pltpu.VMEM((1, D), F32),
            pltpu.VMEM((1, D), F32),
            pltpu.VMEM((1, D), F32),
            pltpu.VMEM((D, D), BF),
            pltpu.VMEM((D, 2 * width), BF),
            pltpu.VMEM((2 * width, D), BF),
            pltpu.VMEM((2 * width, 128), F32),
            pltpu.VMEM((cells, D), BF),
            pltpu.VMEM((4, 8, D), F32),
            pltpu.VMEM((4, 8, D), BF),
            pltpu.VMEM((8, 8, D), BF),
            pltpu.VMEM((D, 256), BF),
            pltpu.VMEM((4, 8, 256), BF),
            pltpu.VMEM((16, 8, 256), BF),
            pltpu.VMEM((4, 3, 1, q_dev), F32),
            pltpu.VMEM((4, outs, q_dev), F32),
            pltpu.VMEM((4, outs, queries), F32),
            pltpu.VMEM((D, queries), BF),
            pltpu.VMEM((width, queries), F32),
            pltpu.VMEM((256, queries), BF),
            pltpu.VMEM((width // HEAD_DIM, 128, queries), F32),
            pltpu.VMEM((width, queries), BF),
            pltpu.VMEM((4, 3 * deep // 2, 128), BF),
            pltpu.VMEM((4, 3 * deep // 2, 128), BF),
            pltpu.VMEM((4, 3 * deep // 2, 128), BF),
            pltpu.VMEM((4, 3 * deep // 2, 128), BF),
            pltpu.VMEM((3 * deep // 2, 128), F32),
            dma((12,)),
            dma((4,)),
            dma((1,)),
            dma((3,)),
            dma((3,)),
            dma((3,)),
            dma((3,)),
            dma((31,)),
            dma((1,)),
            dma((3,)),
            dma((3,)),
            dma((8,)),
            dma((8,)),
        ],
        compiler_params=pltpu.CompilerParams(
            collective_id=0, has_side_effects=True, vmem_limit_bytes=64 * 1024 * 1024 - 256 * 1024
        ),
    )(
        cell_feats[0],
        cell_types,
        cell_routes[0].T,
        positions[0].reshape(3, 1, q_dev),
        targets[0],
        type_weight,
        query_weight,
        key_weight,
        out_weight.T,
        anchor_gain,
        query_gain,
        key_gain,
    )
    predicted, grad = pl.pallas_call(
        finish,
        out_shape=(jax.ShapeDtypeStruct((outs, q_dev), F32), jax.ShapeDtypeStruct((deep, width), F32)),
        in_specs=[vmem, vmem],
        out_specs=(vmem, vmem),
        compiler_params=pltpu.CompilerParams(vmem_limit_bytes=1024 * 1024),
    )(predicted, grad)
    return (predicted[None], grad)


def solution(mesh):
    in_specs = (
        P(("groups", "dp"), ("cells", "ctx"), None),
        P(("groups", "dp"), ("cells", "ctx")),
        P(("groups", "dp"), ("cells", "ctx"), None),
        P(("groups", "dp"), None, ("cells", "ctx")),
        P(("groups", "dp"), None, ("cells", "ctx")),
        P(),
        P(),
        P(),
        P(),
        P(),
        P(),
        P(),
    )
    out_specs = (P(("groups", "dp"), None, ("cells", "ctx")), P(("groups", "cells"), ("ctx", "dp")))
    sizes = mesh.shape
    fits = sizes["groups"] == 1 and sizes["dp"] == 1 and sizes["ctx"] == 4 and sizes["cells"] == 8
    body = fused_device if fits else general_device
    return jax.shard_map(
        body, mesh=mesh, in_specs=in_specs, out_specs=out_specs, check_vma=False
    )
```

time: 32.8 us -> 28.1 us (0.86)
  Pallas kernels: 32 us -> 27.2 us
    pallas_call x1, Pallas kernels: 31.3 us -> 26.5 us  [fused_device(): pl.pallas_call(fused_kernel, out_shape=(pltpu.VMEM((outs, q_dev), F32), p...]
where the time goes in v2:
time: 28.1 us; the launch traced here: 27.8 us
  Pallas kernels  27.2 us (97%)
  between operations  0.64 us (2%)
    pallas_call x1, Pallas kernels, fused_device(): pl.pallas_call(fused_kernel, out_shape=(pltpu.VMEM((outs, q_dev), F32), p...  26.5 us
    pallas_call x1, Pallas kernels, fused_device(): pl.pallas_call(finish, out_shape=(jax.ShapeDtypeStruct((outs, q_dev), F32...  0.65 us

profile of v2, /device:TPU:0, one launch (start us, length us, event | category | flops | bytes accessed | tf_op | source)
XLA Modules:
  0.0 27.8 jit_solution(18032907195136463000)
XLA Ops:
  0.6 26.5 %shard_map.131 = (f32[4,128]{1,0:T(4,128)S(1)}, f32[96,192]{1,0:T(8,128)S(1)}) custom-call(bf16[1024,128]{1,0:T(8,128)(2,1)} %bitcast.8, s32[1,8]{1,0:T(1,128)} %types_h.1, s32[2,1024]{1,0:T(2,128)} %bitcast.9, f32[3,1,128]{2,1,0:T(1,128)} %bitcast.12, f32[4,128]{1,0:T(4,128)} %bitcast.11, bf16[4,128,768]{2,1,0:T(8,128)(2,1)} %type_w_h.1, ...), custom_call_target="tpu_custom_call" | custom-call | tf_op jit(solution)/shard_map/pallas_call | solution.py:632
  27.1 0.7 %shard_map.132 = (f32[4,128]{1,0:T(4,128)}, f32[96,192]{1,0:T(8,128)}) custom-call(f32[4,128]{1,0:T(4,128)S(1)} %get-tuple-element.6.pred_in, f32[96,192]{1,0:T(8,128)S(1)} %get-tuple-element.7.grad_in), custom_call_target="tpu_custom_call" | custom-call | tf_op jit(solution)/shard_map/pallas_call | solution.py:706

commit v3 on v2

--- a/solution.py
+++ b/solution.py
@@ -260,6 +260,7 @@
     o_recv,
     g_send,
     g_recv,
+    ready,
 ):
     c = lax.axis_index("cells")
     x = lax.axis_index("ctx")
@@ -306,8 +307,22 @@
     for load in loads[:4]:
         load.start()
     barrier = pltpu.get_barrier_semaphore()
-    for spot in others:
+    half = z // 2
+    is_owner = (c >= 2) & (c < 6)
+    greeted = [(m, dy, 0, 0) for m in (1, 2) for dy in (0, 1)]
+    greeted += [(0, 1, 0, 0), (0, 0, 1, 0), (0, 1, 1, 0), (0, 0, 0, 1), (0, 0, 1, 1)]
+
+    def greet(spot):
         pl.semaphore_signal(barrier, inc=1, device_id=device(*spot), device_id_type=MESH)
+
+    for spot in greeted:
+        greet(spot)
+
+    @pl.when(is_owner)
+    def _():
+        greet((3, 0, 0, 0))
+        greet((3, 1, 0, 0))
+
     for load in loads[4:]:
         load.start()
 
@@ -340,10 +355,6 @@
     pos_all[place] = pos[...]
     tgt_all[place] = tgt[...]
 
-    half = z // 2
-    is_owner = (c >= 2) & (c < 6)
-    mine = 2 + half * 2 + y
-
     def pool_copy(i):
         dh, dy = ((1, 1), (1, 0), (0, 1), (0, 0))[i]
         o = flip(half, dh) * 2 + flip(y, dy)
@@ -355,13 +366,18 @@
             {"cells": 2 + o, "ctx": x},
         )
 
-    pl.semaphore_wait(barrier, len(others))
+    pl.semaphore_wait(barrier, len(greeted) + jnp.where(is_owner, 2, 0))
     for i in range(3):
         pool_copy(i).start()
 
     @pl.when(jnp.logical_not(is_owner))
     def _():
         pool_copy(3).start()
+
+    @pl.when(is_owner)
+    def _():
+        for dx, dk in ((1, 1), (1, 0), (0, 1)):
+            pl.semaphore_signal(ready, inc=1, device_id=device(0, 0, dx, dk), device_id_type=MESH)
 
     p_copies = []
     t_copies = []
@@ -390,8 +406,6 @@
             emb_t[spot : spot + FREQ, cols] = (series(SIN_TERMS, square) * rest * sign).astype(BF)
             emb_t[spot + FREQ : spot + 2 * FREQ, cols] = (series(COS_TERMS, square) * sign).astype(BF)
 
-    embed_block(place)
-
     out_f = out_wt[...].astype(F32)
     out_t = jnp.concatenate([out_f, jnp.zeros_like(out_f)], axis=0).T.astype(BF)
     lane8 = lax.broadcasted_iota(jnp.int32, (8, 256), 1)
@@ -402,26 +416,6 @@
     keep = (lax.broadcasted_iota(jnp.int32, (D, 256), 0) // HEAD_DIM == head_of) & (inside < heads)
     keep = keep & (lax.rem(lane_d, 64) < 48)
     w_out[...] = jnp.where(keep, mm(out_t, pick), 0.0).astype(BF)
-
-    qwin_t[...] = qwin[...].T
-    gain_t[...] = jnp.broadcast_to(query_g[:, pl.ds(start, pair)], (128, pair)).T
-
-    for i, (dy, dx) in enumerate(quad):
-        p_copies[i].wait_recv()
-        embed_block(flip(y, dy) * 2 + flip(xx, dx))
-
-    rows_mine = pl.ds(pl.multiple_of(y * width, 64), width)
-    qlin[...] = mm(qwin_t[rows_mine, :], emb_t[...])
-    gains = gain_t[rows_mine, :][:, 0:1]
-
-    def norm_of(h):
-        piece = qlin[h * HEAD_DIM : (h + 1) * HEAD_DIM, :]
-        return lax.rsqrt(jnp.mean(piece * piece, axis=0, keepdims=True) + EPS)
-
-    for h in range(heads):
-        rows = slice(h * HEAD_DIM, (h + 1) * HEAD_DIM)
-        hats[rows, :] = (qlin[rows, :] * norm_of(h) * gains[rows, :]).astype(BF)
-    hats[width:, :] = jnp.zeros((256 - width, hats.shape[1]), BF)
 
     def key_copy(i):
         m, dy, dx, dk = others[i]
@@ -460,9 +454,31 @@
             kv_out[g] = jnp.concatenate(
                 [keys[:, width * g : width * g + width], mixed[:, 64 * g : 64 * g + 64]], axis=1
             ).astype(BF)
+        pl.semaphore_wait(ready, 3)
         for i in range(len(others)):
             key_copy(i).start()
         kv_in[(c - 2) * 4 + x] = kv_out[xx * 2 + y]
+
+    embed_block(place)
+    qwin_t[...] = qwin[...].T
+    gain_t[...] = jnp.broadcast_to(query_g[:, pl.ds(start, pair)], (128, pair)).T
+
+    for i, (dy, dx) in enumerate(quad):
+        p_copies[i].wait_recv()
+        embed_block(flip(y, dy) * 2 + flip(xx, dx))
+
+    rows_mine = pl.ds(pl.multiple_of(y * width, 64), width)
+    qlin[...] = mm(qwin_t[rows_mine, :], emb_t[...])
+    gains = gain_t[rows_mine, :][:, 0:1]
+
+    def norm_of(h):
+        piece = qlin[h * HEAD_DIM : (h + 1) * HEAD_DIM, :]
+        return lax.rsqrt(jnp.mean(piece * piece, axis=0, keepdims=True) + EPS)
+
+    for h in range(heads):
+        rows = slice(h * HEAD_DIM, (h + 1) * HEAD_DIM)
+        hats[rows, :] = (qlin[rows, :] * norm_of(h) * gains[rows, :]).astype(BF)
+    hats[width:, :] = jnp.zeros((256 - width, hats.shape[1]), BF)
 
     def keys_arrive(count):
         landed = kv_in.at[pl.ds(0, count)]
@@ -685,6 +701,7 @@
             dma((3,)),
             dma((8,)),
             dma((8,)),
+            pltpu.SemaphoreType.REGULAR,
         ],
         compiler_params=pltpu.CompilerParams(
             collective_id=0, has_side_effects=True, vmem_limit_bytes=64 * 1024 * 1024 - 256 * 1024

time: 28.1 us -> 27.3 us (0.972)
  Pallas kernels: 27.2 us -> 26.5 us
    pallas_call x1, Pallas kernels: 26.5 us -> 25.9 us  [fused_device(): pl.pallas_call(fused_kernel, out_shape=(pltpu.VMEM((outs, q_dev), F32), p...]
where the time goes in v3:
time: 27.3 us; the launch traced here: 27.2 us
  Pallas kernels  26.5 us (97%)
  between operations  0.64 us (2%)
    pallas_call x1, Pallas kernels, fused_device(): pl.pallas_call(fused_kernel, out_shape=(pltpu.VMEM((outs, q_dev), F32), p...  25.9 us
    pallas_call x1, Pallas kernels, fused_device(): pl.pallas_call(finish, out_shape=(jax.ShapeDtypeStruct((outs, q_dev), F32...  0.65 us

profile of v3, /device:TPU:0, one launch (start us, length us, event | category | flops | bytes accessed | tf_op | source)
XLA Modules:
  0.0 27.2 jit_solution(5910302409497310469)
XLA Ops:
  0.6 25.9 %shard_map.131 = (f32[4,128]{1,0:T(4,128)S(1)}, f32[96,192]{1,0:T(8,128)S(1)}) custom-call(bf16[1024,128]{1,0:T(8,128)(2,1)} %bitcast.8, s32[1,8]{1,0:T(1,128)} %types_h.1, s32[2,1024]{1,0:T(2,128)} %bitcast.9, f32[3,1,128]{2,1,0:T(1,128)} %bitcast.12, f32[4,128]{1,0:T(4,128)} %bitcast.11, bf16[4,128,768]{2,1,0:T(8,128)(2,1)} %type_w_h.1, ...), custom_call_target="tpu_custom_call" | custom-call | tf_op jit(solution)/shard_map/pallas_call | solution.py:648
  26.5 0.7 %shard_map.132 = (f32[4,128]{1,0:T(4,128)}, f32[96,192]{1,0:T(8,128)}) custom-call(f32[4,128]{1,0:T(4,128)S(1)} %get-tuple-element.6.pred_in, f32[96,192]{1,0:T(8,128)S(1)} %get-tuple-element.7.grad_in), custom_call_target="tpu_custom_call" | custom-call | tf_op jit(solution)/shard_map/pallas_call | solution.py:723

commit v4 on v3

--- a/solution.py
+++ b/solution.py
@@ -234,8 +234,7 @@
     w_out,
     kv_out,
     kv_in,
-    pos_all,
-    tgt_all,
+    both_all,
     pred_part,
     emb_t,
     qlin,
@@ -252,8 +251,6 @@
     a_recv,
     p_send,
     p_recv,
-    t_send,
-    t_recv,
     k_send,
     k_recv,
     o_send,
@@ -352,8 +349,8 @@
     for o in range(4):
         part[o] = sums[8 * o : 8 * o + 8, :]
         part_b[o] = sums[8 * o : 8 * o + 8, :].astype(BF)
-    pos_all[place] = pos[...]
-    tgt_all[place] = tgt[...]
+    both_all[place, 0:3, :] = pos[:, 0, :]
+    both_all[place, 4:8, :] = tgt[...]
 
     def pool_copy(i):
         dh, dy = ((1, 1), (1, 0), (0, 1), (0, 0))[i]
@@ -380,14 +377,11 @@
             pl.semaphore_signal(ready, inc=1, device_id=device(0, 0, dx, dk), device_id_type=MESH)
 
     p_copies = []
-    t_copies = []
     quad = ((1, 1), (1, 0), (0, 1))
     for i, (dy, dx) in enumerate(quad):
-        p_copies.append(copy_to(pos, pos_all.at[place], p_send.at[i], p_recv.at[i], device(0, dy, dx, 0)))
+        mine = both_all.at[place]
+        p_copies.append(copy_to(mine, mine, p_send.at[i], p_recv.at[i], device(0, dy, dx, 0)))
         p_copies[i].start()
-    for i, (dy, dx) in enumerate(quad):
-        t_copies.append(copy_to(tgt, tgt_all.at[place], t_send.at[i], t_recv.at[i], device(0, dy, dx, 0)))
-        t_copies[i].start()
 
     for load in loads[6:]:
         load.wait()
@@ -396,7 +390,7 @@
     def embed_block(i):
         cols = pl.ds(pl.multiple_of(i * q_dev, 128), q_dev)
         for d in range(3):
-            turns = rates * pos_all[i, d]
+            turns = rates * both_all[i, pl.ds(d, 1), :]
             whole = jnp.floor(turns + 0.5)
             rest = turns - whole
             parity = whole * 0.5
@@ -506,12 +500,13 @@
     queries = qlin.shape[1]
     out_row = lax.broadcasted_iota(jnp.int32, (16, queries), 0) // 4
     by_head = jnp.zeros((16, queries), F32)
+    shares = []
     for h in range(heads):
-        exponent = jnp.exp(mm(lefts[h], hats[(h // 2) * 128 : (h // 2) * 128 + 128, :]) * scale)
-        share = exponent * (1.0 / jnp.sum(exponent, axis=0, keepdims=True))
-        probs[h] = share
-        outs = mm(both_t[width : width + 32, :], share.astype(BF))
-        by_head = jnp.where(out_row == h, outs[:16] + outs[16:], by_head)
+        exponent = jnp.exp2(mm(lefts[h], hats[(h // 2) * 128 : (h // 2) * 128 + 128, :]) * (scale * math.log2(math.e)))
+        probs[h] = exponent
+        shares.append(1.0 / jnp.sum(exponent, axis=0, keepdims=True))
+        outs = mm(both_t[width : width + 32, :], exponent.astype(BF))
+        by_head = jnp.where(out_row == h, (outs[:16] + outs[16:]) * shares[h], by_head)
     pred_part[0] = by_head[0:4] + by_head[4:8] + by_head[8:12]
     o_copies = []
     for i, (dy, dx) in enumerate(quad):
@@ -532,11 +527,11 @@
         for i in range(len(others)):
             key_copy(i).wait_send()
 
-    for copy in p_copies + t_copies:
+    for copy in p_copies:
         copy.wait_send()
-    for copy in t_copies:
-        copy.wait_recv()
-    goals = jnp.concatenate([tgt_all[i] for i in range(4)], axis=1)
+    for h in range(heads):
+        probs[h] = probs[h] * shares[h]
+    goals = jnp.concatenate([both_all[i, 4:8, :] for i in range(4)], axis=1)
     backs = [
         jnp.where((lane >= 64) & (lax.rem(lane, 16) // 4 == h), tile1, 0.0).astype(BF) for h in range(heads)
     ]
@@ -549,74 +544,96 @@
     none = jnp.zeros((64, queries), F32)
     split = jnp.concatenate([none] + [coarse] * 8 + [rest] * 8, axis=0).astype(BF)
     weighed = by_head * jnp.concatenate([residue] * 4, axis=0)
-    for h in range(heads):
-        rows = slice(h * HEAD_DIM, (h + 1) * HEAD_DIM)
-        inner = jnp.sum(weighed[4 * h : 4 * h + 4], axis=0, keepdims=True)
-        grad_s = (probs[h] * (mm(backs[h], split) - inner)).astype(BF)
-        grad_q = mm(both_t[rows, :], grad_s) * scale
-        weighted = grad_q * gains[rows, :]
-        inverse = norm_of(h)
-        unit = qlin[rows, :] * inverse
-        shared = jnp.mean(weighted * unit, axis=0, keepdims=True)
-        glin[rows, :] = ((weighted - unit * shared) * inverse).astype(BF)
-
-    glin_t = glin[...].T
     deep = D // 8
-
-    def terms(slab):
-        rows = pl.ds(pl.multiple_of(slab * deep, 16), deep)
-        full = mm(emb_t[rows, :], glin_t)
-        rest = jnp.concatenate([full[: deep // 2, 128:], full[deep // 2 :, 128:]], axis=1)
-        return jnp.concatenate([full[:, :128], rest], axis=0)
-
-    mates = {}
-    for m in (3, 2, 1, 0):
-        y_send[m] = terms(far_z(m) * 2 + 1 - k).astype(BF)
-        mates[m] = copy_to(y_send.at[m], y_in.at[m], g_send.at[m], g_recv.at[m], device(0, 0, 0, 1))
-        mates[m].start()
-
-    def along(m):
+    tall = deep // 2
+    groups = ((0, 1, 2),)
+    order = (3, 2, 1, 0)
+
+    def blocks(group, side):
+        slabs = [emb_t[pl.ds(pl.multiple_of((far_z(m) * 2 + side) * deep, 16), deep), :] for m in order]
+        cols = glin[group[0] * HEAD_DIM : (group[-1] + 1) * HEAD_DIM, :]
+        full = lax.dot_general(
+            jnp.concatenate(slabs, axis=0), cols, (((1,), (1,)), ((), ())), preferred_element_type=F32
+        )
+        packed = {}
+        for i, m in enumerate(order):
+            for j, h in enumerate(group):
+                piece = full[deep * i : deep * i + deep, HEAD_DIM * j : HEAD_DIM * j + HEAD_DIM]
+                packed[m, h] = jnp.concatenate([piece[:tall], piece[tall:]], axis=1)
+        return packed
+
+    def to_mate(g):
+        span = pl.ds(groups[g][0], len(groups[g]))
+        return copy_to(y_send.at[span], y_in.at[span], g_send.at[g], g_recv.at[g], device(0, 0, 0, 1))
+
+    def along(g, m):
+        span = pl.ds(groups[g][0], len(groups[g]))
         peer = {"cells": far_z(m) * 2 + k, "ctx": xx * 2 + y}
-        return copy_to(z_send.at[m], z_in.at[m], g_send.at[4 + m], g_recv.at[4 + m], peer)
-
-    for m in (3, 2, 1):
-        mixed = terms(far_z(m) * 2 + k)
-        mates[m].wait_recv()
-        z_send[m] = (mixed + y_in[m].astype(F32)).astype(BF)
-        along(m).start()
-    mixed = terms(z * 2 + k)
-    mates[0].wait_recv()
-    mixed = mixed + y_in[0].astype(F32)
-    total[...] = mixed
-
-    @pl.when(y != k)
-    def _():
-        z_send[0] = mixed.astype(BF)
-        along(0).start()
+        spot = 3 + 4 * g + m
+        return copy_to(z_send.at[m, span], z_in.at[m, span], g_send.at[spot], g_recv.at[spot], peer)
+
+    for g, group in enumerate(groups):
+        for h in group:
+            rows = slice(h * HEAD_DIM, (h + 1) * HEAD_DIM)
+            inner = jnp.sum(weighed[4 * h : 4 * h + 4], axis=0, keepdims=True)
+            grad_s = (probs[h] * (mm(backs[h], split) - inner)).astype(BF)
+            weighted = mm(both_t[rows, :], grad_s) * (gains[rows, :] * scale)
+            inverse = norm_of(h)
+            unit = qlin[rows, :] * inverse
+            shared = jnp.mean(weighted * unit, axis=0, keepdims=True)
+            glin[rows, :] = ((weighted - unit * shared) * inverse).astype(BF)
+        packed = blocks(group, 1 - k)
+        for m in order:
+            for h in group:
+                y_send[h, m] = packed[m, h].astype(BF)
+        to_mate(g).start()
+    kept = [blocks(group, k) for group in groups]
+    for g, group in enumerate(groups):
+        to_mate(g).wait_recv()
+        for m in order[:3]:
+            for h in group:
+                z_send[m, h] = (kept[g][m, h] + y_in[h, m].astype(F32)).astype(BF)
+            along(g, m).start()
+        for h in group:
+            near = kept[g][0, h] + y_in[h, 0].astype(F32)
+            total[h] = near
+            z_send[0, h] = near.astype(BF)
+
+        @pl.when(y != k)
+        def _():
+            along(g, 0).start()
 
     cols = pl.ds(pl.multiple_of(place * q_dev, 128), q_dev)
     for copy in o_copies:
         copy.wait_send()
     pred_part[0] = predicted
     pred_out[...] = pred_part[0, :, cols]
-    for m in (3, 2, 1, 0):
-        mates[m].wait_send()
-
-    @pl.when(y != k)
-    def _():
-        along(0).wait_recv()
-        total[...] = z_in[0].astype(F32)
-        along(0).wait_send()
-
-    summed = total[...]
-    for m in (1, 2, 3):
-        along(m).wait_recv()
-        summed = summed + z_in[m].astype(F32)
-    grad_out[:, :128] = summed[:deep]
-    grad_out[: deep // 2, 128:] = summed[deep:, : width - 128]
-    grad_out[deep // 2 :, 128:] = summed[deep:, width - 128 :]
-    for m in (1, 2, 3):
-        along(m).wait_send()
+    for g in range(len(groups)):
+        to_mate(g).wait_send()
+    for g, group in enumerate(groups):
+
+        @pl.when(y != k)
+        def _():
+            along(g, 0).wait_recv()
+            for h in group:
+                total[h] = z_in[0, h].astype(F32)
+
+        for m in (1, 2, 3):
+            along(g, m).wait_recv()
+        for h in group:
+            summed = total[h]
+            for m in (1, 2, 3):
+                summed = summed + z_in[m, h].astype(F32)
+            spot = slice(h * HEAD_DIM, (h + 1) * HEAD_DIM)
+            grad_out[:tall, spot] = summed[:, :HEAD_DIM]
+            grad_out[tall:, spot] = summed[:, HEAD_DIM:]
+    for g in range(len(groups)):
+        for m in (1, 2, 3):
+            along(g, m).wait_send()
+
+        @pl.when(y != k)
+        def _():
+            along(g, 0).wait_send()
 
 
 def finish(pred_in, grad_in, pred_o, grad_o):
@@ -675,32 +692,29 @@
             pltpu.VMEM((D, 256), BF),
             pltpu.VMEM((4, 8, 256), BF),
             pltpu.VMEM((16, 8, 256), BF),
-            pltpu.VMEM((4, 3, 1, q_dev), F32),
-            pltpu.VMEM((4, outs, q_dev), F32),
+            pltpu.VMEM((4, 8, q_dev), F32),
             pltpu.VMEM((4, outs, queries), F32),
             pltpu.VMEM((D, queries), BF),
             pltpu.VMEM((width, queries), F32),
             pltpu.VMEM((256, queries), BF),
             pltpu.VMEM((width // HEAD_DIM, 128, queries), F32),
             pltpu.VMEM((width, queries), BF),
-            pltpu.VMEM((4, 3 * deep // 2, 128), BF),
-            pltpu.VMEM((4, 3 * deep // 2, 128), BF),
-            pltpu.VMEM((4, 3 * deep // 2, 128), BF),
-            pltpu.VMEM((4, 3 * deep // 2, 128), BF),
-            pltpu.VMEM((3 * deep // 2, 128), F32),
+            pltpu.VMEM((3, 4, deep // 2, 128), BF),
+            pltpu.VMEM((3, 4, deep // 2, 128), BF),
+            pltpu.VMEM((4, 3, deep // 2, 128), BF),
+            pltpu.VMEM((4, 3, deep // 2, 128), BF),
+            pltpu.VMEM((3, deep // 2, 128), F32),
             dma((12,)),
             dma((4,)),
             dma((1,)),
-            dma((3,)),
-            dma((3,)),
             dma((3,)),
             dma((3,)),
             dma((31,)),
             dma((1,)),
             dma((3,)),
             dma((3,)),
-            dma((8,)),
-            dma((8,)),
+            dma((15,)),
+            dma((15,)),
             pltpu.SemaphoreType.REGULAR,
         ],
         compiler_params=pltpu.CompilerParams(

time: 27.3 us -> 26.1 us (0.956)
  Pallas kernels: 26.5 us -> 25.3 us
    pallas_call x1, Pallas kernels: 25.9 us -> 24.7 us  [fused_device(): pl.pallas_call(fused_kernel, out_shape=(pltpu.VMEM((outs, q_dev), F32), p...]
where the time goes in v4:
time: 26.1 us; the launch traced here: 26 us
  Pallas kernels  25.3 us (97%)
  between operations  0.64 us (2%)
    pallas_call x1, Pallas kernels, fused_device(): pl.pallas_call(fused_kernel, out_shape=(pltpu.VMEM((outs, q_dev), F32), p...  24.7 us
    pallas_call x1, Pallas kernels, fused_device(): pl.pallas_call(finish, out_shape=(jax.ShapeDtypeStruct((outs, q_dev), F32...  0.65 us

profile of v4, /device:TPU:0, one launch (start us, length us, event | category | flops | bytes accessed | tf_op | source)
XLA Modules:
  0.0 26.0 jit_solution(563498959165787218)
XLA Ops:
  0.6 24.7 %shard_map.131 = (f32[4,128]{1,0:T(4,128)S(1)}, f32[96,192]{1,0:T(8,128)S(1)}) custom-call(bf16[1024,128]{1,0:T(8,128)(2,1)} %bitcast.8, s32[1,8]{1,0:T(1,128)} %types_h.1, s32[2,1024]{1,0:T(2,128)} %bitcast.9, f32[3,1,128]{2,1,0:T(1,128)} %bitcast.12, f32[4,128]{1,0:T(4,128)} %bitcast.11, bf16[4,128,768]{2,1,0:T(8,128)(2,1)} %type_w_h.1, ...), custom_call_target="tpu_custom_call" | custom-call | tf_op jit(solution)/shard_map/pallas_call | solution.py:665
  25.3 0.7 %shard_map.132 = (f32[4,128]{1,0:T(4,128)}, f32[96,192]{1,0:T(8,128)}) custom-call(f32[4,128]{1,0:T(4,128)S(1)} %get-tuple-element.6.pred_in, f32[96,192]{1,0:T(8,128)S(1)} %get-tuple-element.7.grad_in), custom_call_target="tpu_custom_call" | custom-call | tf_op jit(solution)/shard_map/pallas_call | solution.py:737

commit v5 on v3

--- a/solution.py
+++ b/solution.py
@@ -234,8 +234,7 @@
     w_out,
     kv_out,
     kv_in,
-    pos_all,
-    tgt_all,
+    both_all,
     pred_part,
     emb_t,
     qlin,
@@ -252,8 +251,6 @@
     a_recv,
     p_send,
     p_recv,
-    t_send,
-    t_recv,
     k_send,
     k_recv,
     o_send,
@@ -352,8 +349,8 @@
     for o in range(4):
         part[o] = sums[8 * o : 8 * o + 8, :]
         part_b[o] = sums[8 * o : 8 * o + 8, :].astype(BF)
-    pos_all[place] = pos[...]
-    tgt_all[place] = tgt[...]
+    both_all[place, 0:3, :] = pos[:, 0, :]
+    both_all[place, 4:8, :] = tgt[...]
 
     def pool_copy(i):
         dh, dy = ((1, 1), (1, 0), (0, 1), (0, 0))[i]
@@ -380,14 +377,11 @@
             pl.semaphore_signal(ready, inc=1, device_id=device(0, 0, dx, dk), device_id_type=MESH)
 
     p_copies = []
-    t_copies = []
     quad = ((1, 1), (1, 0), (0, 1))
     for i, (dy, dx) in enumerate(quad):
-        p_copies.append(copy_to(pos, pos_all.at[place], p_send.at[i], p_recv.at[i], device(0, dy, dx, 0)))
+        mine = both_all.at[place]
+        p_copies.append(copy_to(mine, mine, p_send.at[i], p_recv.at[i], device(0, dy, dx, 0)))
         p_copies[i].start()
-    for i, (dy, dx) in enumerate(quad):
-        t_copies.append(copy_to(tgt, tgt_all.at[place], t_send.at[i], t_recv.at[i], device(0, dy, dx, 0)))
-        t_copies[i].start()
 
     for load in loads[6:]:
         load.wait()
@@ -396,7 +390,7 @@
     def embed_block(i):
         cols = pl.ds(pl.multiple_of(i * q_dev, 128), q_dev)
         for d in range(3):
-            turns = rates * pos_all[i, d]
+            turns = rates * both_all[i, pl.ds(d, 1), :]
             whole = jnp.floor(turns + 0.5)
             rest = turns - whole
             parity = whole * 0.5
@@ -417,8 +411,10 @@
     keep = keep & (lax.rem(lane_d, 64) < 48)
     w_out[...] = jnp.where(keep, mm(out_t, pick), 0.0).astype(BF)
 
+    by_hops = sorted(others, key=lambda spot: -((0, 1, 2, 1)[spot[0]] * 2 + spot[1] * 2 + spot[2] * 2 + spot[3]))
+
     def key_copy(i):
-        m, dy, dx, dk = others[i]
+        m, dy, dx, dk = by_hops[i]
         group = flip(xx, dx) * 2 + flip(y, dy)
         return copy_to(
             kv_out.at[group],
@@ -506,12 +502,13 @@
     queries = qlin.shape[1]
     out_row = lax.broadcasted_iota(jnp.int32, (16, queries), 0) // 4
     by_head = jnp.zeros((16, queries), F32)
+    shares = []
     for h in range(heads):
-        exponent = jnp.exp(mm(lefts[h], hats[(h // 2) * 128 : (h // 2) * 128 + 128, :]) * scale)
-        share = exponent * (1.0 / jnp.sum(exponent, axis=0, keepdims=True))
-        probs[h] = share
-        outs = mm(both_t[width : width + 32, :], share.astype(BF))
-        by_head = jnp.where(out_row == h, outs[:16] + outs[16:], by_head)
+        exponent = jnp.exp2(mm(lefts[h], hats[(h // 2) * 128 : (h // 2) * 128 + 128, :]) * (scale * math.log2(math.e)))
+        probs[h] = exponent
+        shares.append(1.0 / jnp.sum(exponent, axis=0, keepdims=True))
+        outs = mm(both_t[width : width + 32, :], exponent.astype(BF))
+        by_head = jnp.where(out_row == h, (outs[:16] + outs[16:]) * shares[h], by_head)
     pred_part[0] = by_head[0:4] + by_head[4:8] + by_head[8:12]
     o_copies = []
     for i, (dy, dx) in enumerate(quad):
@@ -532,11 +529,11 @@
         for i in range(len(others)):
             key_copy(i).wait_send()
 
-    for copy in p_copies + t_copies:
+    for copy in p_copies:
         copy.wait_send()
-    for copy in t_copies:
-        copy.wait_recv()
-    goals = jnp.concatenate([tgt_all[i] for i in range(4)], axis=1)
+    for h in range(heads):
+        probs[h] = probs[h] * shares[h]
+    goals = jnp.concatenate([both_all[i, 4:8, :] for i in range(4)], axis=1)
     backs = [
         jnp.where((lane >= 64) & (lax.rem(lane, 16) // 4 == h), tile1, 0.0).astype(BF) for h in range(heads)
     ]
@@ -553,70 +550,88 @@
         rows = slice(h * HEAD_DIM, (h + 1) * HEAD_DIM)
         inner = jnp.sum(weighed[4 * h : 4 * h + 4], axis=0, keepdims=True)
         grad_s = (probs[h] * (mm(backs[h], split) - inner)).astype(BF)
-        grad_q = mm(both_t[rows, :], grad_s) * scale
-        weighted = grad_q * gains[rows, :]
+        weighted = mm(both_t[rows, :], grad_s) * (gains[rows, :] * scale)
         inverse = norm_of(h)
         unit = qlin[rows, :] * inverse
         shared = jnp.mean(weighted * unit, axis=0, keepdims=True)
         glin[rows, :] = ((weighted - unit * shared) * inverse).astype(BF)
 
-    glin_t = glin[...].T
     deep = D // 8
-
-    def terms(slab):
-        rows = pl.ds(pl.multiple_of(slab * deep, 16), deep)
-        full = mm(emb_t[rows, :], glin_t)
-        rest = jnp.concatenate([full[: deep // 2, 128:], full[deep // 2 :, 128:]], axis=1)
-        return jnp.concatenate([full[:, :128], rest], axis=0)
-
-    mates = {}
-    for m in (3, 2, 1, 0):
-        y_send[m] = terms(far_z(m) * 2 + 1 - k).astype(BF)
-        mates[m] = copy_to(y_send.at[m], y_in.at[m], g_send.at[m], g_recv.at[m], device(0, 0, 0, 1))
-        mates[m].start()
-
-    def along(m):
-        peer = {"cells": far_z(m) * 2 + k, "ctx": xx * 2 + y}
-        return copy_to(z_send.at[m], z_in.at[m], g_send.at[4 + m], g_recv.at[4 + m], peer)
-
-    for m in (3, 2, 1):
-        mixed = terms(far_z(m) * 2 + k)
-        mates[m].wait_recv()
-        z_send[m] = (mixed + y_in[m].astype(F32)).astype(BF)
-        along(m).start()
-    mixed = terms(z * 2 + k)
-    mates[0].wait_recv()
-    mixed = mixed + y_in[0].astype(F32)
-    total[...] = mixed
+    tall = deep // 2
+    middle = (z == 1) | (z == 2)
+    places = [jnp.where(middle, a, b) for a, b in ((2, 3), (1, 2), (3, 1))]
+    layers = [jnp.where(middle, far_z(a), far_z(b)) for a, b in ((2, 3), (1, 2), (3, 1))] + [z]
+
+    def blocks(side, steps):
+        slabs = [emb_t[pl.ds(pl.multiple_of((layers[j] * 2 + side) * deep, 16), deep), :] for j in steps]
+        full = lax.dot_general(
+            jnp.concatenate(slabs, axis=0), glin[...], (((1,), (1,)), ((), ())), preferred_element_type=F32
+        )
+        packed = {}
+        for i, j in enumerate(steps):
+            pieces = []
+            for h in range(heads):
+                piece = full[deep * i : deep * i + deep, HEAD_DIM * h : HEAD_DIM * h + HEAD_DIM]
+                pieces.append(jnp.concatenate([piece[:tall], piece[tall:]], axis=1))
+            packed[j] = jnp.concatenate(pieces, axis=0)
+        return packed
+
+    sent_blocks = blocks(1 - k, (0, 1, 2, 3))
+    for j in range(4):
+        y_send[j] = sent_blocks[j].astype(BF)
+    to_mate = copy_to(y_send, y_in, g_send.at[4], g_recv.at[4], device(0, 0, 0, 1))
+    to_mate.start()
+
+    def along(j):
+        slot = 0 if j == 3 else places[j]
+        peer = {"cells": layers[j] * 2 + k, "ctx": xx * 2 + y}
+        return copy_to(z_send.at[j], z_in.at[slot], g_send.at[j], g_recv.at[slot], peer)
+
+    kept = blocks(k, (0,))
+    to_mate.wait_recv()
+    z_send[0] = (kept[0] + y_in[0].astype(F32)).astype(BF)
+    along(0).start()
+    kept = blocks(k, (1, 2, 3))
+    for j in (1, 2):
+        z_send[j] = (kept[j] + y_in[j].astype(F32)).astype(BF)
+        along(j).start()
+    near = kept[3] + y_in[3].astype(F32)
+    total[...] = near
 
     @pl.when(y != k)
     def _():
-        z_send[0] = mixed.astype(BF)
-        along(0).start()
+        z_send[3] = near.astype(BF)
+        along(3).start()
 
     cols = pl.ds(pl.multiple_of(place * q_dev, 128), q_dev)
     for copy in o_copies:
         copy.wait_send()
     pred_part[0] = predicted
     pred_out[...] = pred_part[0, :, cols]
-    for m in (3, 2, 1, 0):
-        mates[m].wait_send()
+    to_mate.wait_send()
+
+    def arrived(slot):
+        return copy_to(z_send.at[0], z_in.at[slot], g_send.at[0], g_recv.at[slot], device(0, 0, 0, 1))
 
     @pl.when(y != k)
     def _():
-        along(0).wait_recv()
+        arrived(0).wait_recv()
         total[...] = z_in[0].astype(F32)
-        along(0).wait_send()
 
     summed = total[...]
-    for m in (1, 2, 3):
-        along(m).wait_recv()
-        summed = summed + z_in[m].astype(F32)
-    grad_out[:, :128] = summed[:deep]
-    grad_out[: deep // 2, 128:] = summed[deep:, : width - 128]
-    grad_out[deep // 2 :, 128:] = summed[deep:, width - 128 :]
-    for m in (1, 2, 3):
-        along(m).wait_send()
+    for slot in (1, 2, 3):
+        arrived(slot).wait_recv()
+        summed = summed + z_in[slot].astype(F32)
+    for h in range(heads):
+        spot = slice(h * HEAD_DIM, (h + 1) * HEAD_DIM)
+        grad_out[:tall, spot] = summed[tall * h : tall * h + tall, :HEAD_DIM]
+        grad_out[tall:, spot] = summed[tall * h : tall * h + tall, HEAD_DIM:]
+    for j in range(3):
+        along(j).wait_send()
+
+    @pl.when(y != k)
+    def _():
+        along(3).wait_send()
 
 
 def finish(pred_in, grad_in, pred_o, grad_o):
@@ -675,8 +690,7 @@
             pltpu.VMEM((D, 256), BF),
             pltpu.VMEM((4, 8, 256), BF),
             pltpu.VMEM((16, 8, 256), BF),
-            pltpu.VMEM((4, 3, 1, q_dev), F32),
-            pltpu.VMEM((4, outs, q_dev), F32),
+            pltpu.VMEM((4, 8, q_dev), F32),
             pltpu.VMEM((4, outs, queries), F32),
             pltpu.VMEM((D, queries), BF),
             pltpu.VMEM((width, queries), F32),
@@ -693,14 +707,12 @@
             dma((1,)),
             dma((3,)),
             dma((3,)),
-            dma((3,)),
-            dma((3,)),
             dma((31,)),
             dma((1,)),
             dma((3,)),
             dma((3,)),
-            dma((8,)),
-            dma((8,)),
+            dma((5,)),
+            dma((5,)),
             pltpu.SemaphoreType.REGULAR,
         ],
         compiler_params=pltpu.CompilerParams(

time: 27.3 us -> 25.5 us (0.934)
  Pallas kernels: 26.5 us -> 24.7 us
    pallas_call x1, Pallas kernels: 25.9 us -> 24.1 us  [fused_device(): pl.pallas_call(fused_kernel, out_shape=(pltpu.VMEM((outs, q_dev), F32), p...]
where the time goes in v5:
time: 25.5 us; the launch traced here: 25.4 us
  Pallas kernels  24.7 us (97%)
  between operations  0.64 us (3%)
    pallas_call x1, Pallas kernels, fused_device(): pl.pallas_call(fused_kernel, out_shape=(pltpu.VMEM((outs, q_dev), F32), p...  24.1 us
    pallas_call x1, Pallas kernels, fused_device(): pl.pallas_call(finish, out_shape=(jax.ShapeDtypeStruct((outs, q_dev), F32...  0.65 us

profile of v5, /device:TPU:0, one launch (start us, length us, event | category | flops | bytes accessed | tf_op | source)
XLA Modules:
  0.0 25.4 jit_solution(605988070341298011)
XLA Ops:
  0.6 24.1 %shard_map.131 = (f32[4,128]{1,0:T(4,128)S(1)}, f32[96,192]{1,0:T(8,128)S(1)}) custom-call(bf16[1024,128]{1,0:T(8,128)(2,1)} %bitcast.8, s32[1,8]{1,0:T(1,128)} %types_h.1, s32[2,1024]{1,0:T(2,128)} %bitcast.9, f32[3,1,128]{2,1,0:T(1,128)} %bitcast.12, f32[4,128]{1,0:T(4,128)} %bitcast.11, bf16[4,128,768]{2,1,0:T(8,128)(2,1)} %type_w_h.1, ...), custom_call_target="tpu_custom_call" | custom-call | tf_op jit(solution)/shard_map/pallas_call | solution.py:663
  24.7 0.7 %shard_map.132 = (f32[4,128]{1,0:T(4,128)}, f32[96,192]{1,0:T(8,128)}) custom-call(f32[4,128]{1,0:T(4,128)S(1)} %get-tuple-element.6.pred_in, f32[96,192]{1,0:T(8,128)S(1)} %get-tuple-element.7.grad_in), custom_call_target="tpu_custom_call" | custom-call | tf_op jit(solution)/shard_map/pallas_call | solution.py:735

commit v6 on v5

--- a/solution.py
+++ b/solution.py
@@ -239,6 +239,9 @@
     emb_t,
     qlin,
     hats,
+    unit,
+    wide,
+    lean,
     probs,
     glin,
     y_send,
@@ -305,20 +308,29 @@
         load.start()
     barrier = pltpu.get_barrier_semaphore()
     half = z // 2
-    is_owner = (c >= 2) & (c < 6)
-    greeted = [(m, dy, 0, 0) for m in (1, 2) for dy in (0, 1)]
-    greeted += [(0, 1, 0, 0), (0, 0, 1, 0), (0, 1, 1, 0), (0, 0, 0, 1), (0, 0, 1, 1)]
-
-    def greet(spot):
-        pl.semaphore_signal(barrier, inc=1, device_id=device(*spot), device_id_type=MESH)
-
-    for spot in greeted:
-        greet(spot)
+    is_owner = (c >= 2) & (c < 6) & (k == 1)
+
+    def greet(peer):
+        pl.semaphore_signal(barrier, inc=1, device_id=peer, device_id_type=MESH)
+
+    def owner_at(dh, dy):
+        return flip(half, dh) * 2 + flip(y, dy)
 
     @pl.when(is_owner)
     def _():
-        greet((3, 0, 0, 0))
-        greet((3, 1, 0, 0))
+        for m in (2, 3, 1, 0):
+            for dy in (1, 0):
+                for dk in (1, 0):
+                    if m or dy or dk:
+                        greet(device(m, dy, 0, dk))
+
+    @pl.when(jnp.logical_not(is_owner))
+    def _():
+        for dh, dy in ((1, 1), (1, 0), (0, 1), (0, 0)):
+            greet({"cells": 2 + owner_at(dh, dy), "ctx": xx * 2 + 1})
+
+    for dy, dx in ((1, 1), (1, 0), (0, 1)):
+        greet(device(0, dy, dx, 0))
 
     for load in loads[4:]:
         load.start()
@@ -354,16 +366,16 @@
 
     def pool_copy(i):
         dh, dy = ((1, 1), (1, 0), (0, 1), (0, 0))[i]
-        o = flip(half, dh) * 2 + flip(y, dy)
+        o = owner_at(dh, dy)
         return copy_to(
             part_b.at[o],
-            part_in.at[lax.rem(c - (2 + o) + 8, 8)],
+            part_in.at[k * 8 + lax.rem(c - (2 + o) + 8, 8)],
             a_send.at[i],
             a_recv.at[0],
-            {"cells": 2 + o, "ctx": x},
-        )
-
-    pl.semaphore_wait(barrier, len(greeted) + jnp.where(is_owner, 2, 0))
+            {"cells": 2 + o, "ctx": xx * 2 + 1},
+        )
+
+    pl.semaphore_wait(barrier, 3 + jnp.where(is_owner, 15, 4))
     for i in range(3):
         pool_copy(i).start()
 
@@ -373,8 +385,7 @@
 
     @pl.when(is_owner)
     def _():
-        for dx, dk in ((1, 1), (1, 0), (0, 1)):
-            pl.semaphore_signal(ready, inc=1, device_id=device(0, 0, dx, dk), device_id_type=MESH)
+        pl.semaphore_signal(ready, inc=1, device_id=device(0, 0, 1, 0), device_id_type=MESH)
 
     p_copies = []
     quad = ((1, 1), (1, 0), (0, 1))
@@ -418,24 +429,26 @@
         group = flip(xx, dx) * 2 + flip(y, dy)
         return copy_to(
             kv_out.at[group],
-            kv_in.at[(c - 2) * 4 + x],
+            kv_in.at[(c - 2) * 2 + xx],
             k_send.at[i],
-            k_recv.at[0],
+            k_recv.at[half],
             device(m, dy, dx, dk),
         )
 
     @pl.when(is_owner)
     def _():
-        arrived = part_in.at[pl.ds(1, 7)]
+        arrived = part_in.at[pl.ds(0, 15)]
         copy_to(arrived, arrived, a_send.at[0], a_recv.at[0], {"cells": c, "ctx": x}).wait_recv()
-        pooled = part[c - 2]
+        first, second = part_in[0].astype(F32), part[c - 2]
         for s in range(1, 8):
-            pooled = pooled + part_in[s].astype(F32)
+            first = first + part_in[s].astype(F32)
+            second = second + part_in[8 + s].astype(F32)
+        pooled = jnp.concatenate([first, second], axis=0)
+        scaled = (pooled * anchor_g[...]).astype(BF)
         inverse = lax.rsqrt(jnp.mean(pooled * pooled, axis=1, keepdims=True) + EPS)
-        anchors = (pooled * inverse * anchor_g[...]).astype(BF)
-        key_lin = mm(anchors, key_w[...])
-        out_lin = mm(anchors, w_out[...])
-        low = lax.broadcasted_iota(jnp.int32, (8, 128), 1) < HEAD_DIM
+        key_lin = mm(scaled, key_w[...]) * inverse
+        out_lin = mm(scaled, w_out[...]) * inverse
+        low = lax.broadcasted_iota(jnp.int32, (16, 128), 1) < HEAD_DIM
         pieces = []
         for j in range(D // 128):
             piece = key_lin[:, 128 * j : 128 * j + 128]
@@ -445,15 +458,15 @@
             pieces.append(piece * lax.rsqrt(jnp.where(low, first, second) * (1.0 / HEAD_DIM) + EPS))
         keys = jnp.concatenate(pieces, axis=1) * key_g[...]
         coarse = out_lin.astype(BF).astype(F32)
-        mixed = jnp.where(lax.rem(lane8, 64) // 16 == 1, out_lin - coarse, coarse)
+        mixed = jnp.where(lax.rem(lax.broadcasted_iota(jnp.int32, (16, 256), 1), 64) // 16 == 1, out_lin - coarse, coarse)
         for g in range(4):
             kv_out[g] = jnp.concatenate(
                 [keys[:, width * g : width * g + width], mixed[:, 64 * g : 64 * g + 64]], axis=1
             ).astype(BF)
-        pl.semaphore_wait(ready, 3)
+        pl.semaphore_wait(ready, 1)
         for i in range(len(others)):
             key_copy(i).start()
-        kv_in[(c - 2) * 4 + x] = kv_out[xx * 2 + y]
+        kv_in[(c - 2) * 2 + xx] = kv_out[xx * 2 + y]
 
     embed_block(place)
     qwin_t[...] = qwin[...].T
@@ -476,39 +489,51 @@
         hats[rows, :] = (qlin[rows, :] * norm_of(h) * gains[rows, :]).astype(BF)
     hats[width:, :] = jnp.zeros((256 - width, hats.shape[1]), BF)
 
-    def keys_arrive(count):
+    def keys_arrive(part_of, count):
         landed = kv_in.at[pl.ds(0, count)]
-        copy_to(landed, landed, k_send.at[0], k_recv.at[0], {"cells": c, "ctx": x}).wait_recv()
+        copy_to(landed, landed, k_send.at[0], k_recv.at[part_of], {"cells": c, "ctx": x}).wait_recv()
+
+    scale = HEAD_DIM ** (-0.5)
+    lane = lax.broadcasted_iota(jnp.int32, (64, 128), 1)
+    queries = qlin.shape[1]
+
+    def attend(part_of, spot):
+        found = jnp.concatenate([kv_in[part_of * 4 + s].astype(F32) for s in range(4)], axis=0)
+        tile0, tile1 = found[:, :128], found[:, 128:]
+        lefts = [
+            jnp.where(lane < HEAD_DIM, tile0, 0.0).astype(BF),
+            jnp.where(lane >= HEAD_DIM, tile0, 0.0).astype(BF),
+            jnp.where(lane < HEAD_DIM, tile1, 0.0).astype(BF),
+        ]
+        out_cols = tile1.astype(BF).T[64:96, :]
+        tops, outs = [], []
+        for h in range(heads):
+            exponent = jnp.exp2(
+                mm(lefts[h], hats[(h // 2) * 128 : (h // 2) * 128 + 128, :]) * (scale * math.log2(math.e))
+            )
+            probs[h, spot : spot + 64, :] = exponent
+            tops.append(jnp.sum(exponent, axis=0, keepdims=True))
+            both_outs = mm(out_cols, exponent.astype(BF))
+            outs.append(both_outs[:16] + both_outs[16:])
+        return found, tops, outs
 
     @pl.when(is_owner)
     def _():
-        keys_arrive(15)
+        keys_arrive(half, 3)
 
     @pl.when(jnp.logical_not(is_owner))
     def _():
-        keys_arrive(16)
-
-    both_f = jnp.concatenate([kv_in[s].astype(F32) for s in range(16)], axis=0)
-    both = both_f.astype(BF)
-    both_t = both.T
-    scale = HEAD_DIM ** (-0.5)
-    lane = lax.broadcasted_iota(jnp.int32, (both.shape[0], 128), 1)
-    tile0, tile1 = both_f[:, :128], both_f[:, 128:]
-    lefts = [
-        jnp.where(lane < HEAD_DIM, tile0, 0.0).astype(BF),
-        jnp.where(lane >= HEAD_DIM, tile0, 0.0).astype(BF),
-        jnp.where(lane < HEAD_DIM, tile1, 0.0).astype(BF),
-    ]
-    queries = qlin.shape[1]
+        keys_arrive(half, 4)
+
+    near_f, near_tops, near_outs = attend(half, 0)
+    keys_arrive(1 - half, 4)
+    far_f, far_tops, far_outs = attend(1 - half, 64)
     out_row = lax.broadcasted_iota(jnp.int32, (16, queries), 0) // 4
     by_head = jnp.zeros((16, queries), F32)
     shares = []
     for h in range(heads):
-        exponent = jnp.exp2(mm(lefts[h], hats[(h // 2) * 128 : (h // 2) * 128 + 128, :]) * (scale * math.log2(math.e)))
-        probs[h] = exponent
-        shares.append(1.0 / jnp.sum(exponent, axis=0, keepdims=True))
-        outs = mm(both_t[width : width + 32, :], exponent.astype(BF))
-        by_head = jnp.where(out_row == h, (outs[:16] + outs[16:]) * shares[h], by_head)
+        shares.append(1.0 / (near_tops[h] + far_tops[h]))
+        by_head = jnp.where(out_row == h, (near_outs[h] + far_outs[h]) * shares[h], by_head)
     pred_part[0] = by_head[0:4] + by_head[4:8] + by_head[8:12]
     o_copies = []
     for i, (dy, dx) in enumerate(quad):
@@ -534,9 +559,20 @@
     for h in range(heads):
         probs[h] = probs[h] * shares[h]
     goals = jnp.concatenate([both_all[i, 4:8, :] for i in range(4)], axis=1)
+    both_f = jnp.concatenate([near_f, far_f], axis=0)
+    both_t = both_f.astype(BF).T
+    tile1 = both_f[:, 128:]
+    lane = lax.broadcasted_iota(jnp.int32, tile1.shape, 1)
     backs = [
         jnp.where((lane >= 64) & (lax.rem(lane, 16) // 4 == h), tile1, 0.0).astype(BF) for h in range(heads)
     ]
+    for h in range(heads):
+        rows = slice(h * HEAD_DIM, (h + 1) * HEAD_DIM)
+        inverse = norm_of(h)
+        unit_rows = qlin[rows, :] * inverse
+        unit[rows, :] = unit_rows
+        wide[rows, :] = (gains[rows, :] * scale) * inverse
+        lean[rows, :] = (gains[rows, :] * (scale / HEAD_DIM)) * (unit_rows * inverse)
     for copy in o_copies:
         copy.wait_recv()
     predicted = pred_part[0] + pred_part[1] + pred_part[2] + pred_part[3]
@@ -550,11 +586,9 @@
         rows = slice(h * HEAD_DIM, (h + 1) * HEAD_DIM)
         inner = jnp.sum(weighed[4 * h : 4 * h + 4], axis=0, keepdims=True)
         grad_s = (probs[h] * (mm(backs[h], split) - inner)).astype(BF)
-        weighted = mm(both_t[rows, :], grad_s) * (gains[rows, :] * scale)
-        inverse = norm_of(h)
-        unit = qlin[rows, :] * inverse
-        shared = jnp.mean(weighted * unit, axis=0, keepdims=True)
-        glin[rows, :] = ((weighted - unit * shared) * inverse).astype(BF)
+        grad_q = mm(both_t[rows, :], grad_s)
+        shared = jnp.sum(grad_q * lean[rows, :], axis=0, keepdims=True)
+        glin[rows, :] = (grad_q * wide[rows, :] - unit[rows, :] * shared).astype(BF)
 
     deep = D // 8
     tall = deep // 2
@@ -609,6 +643,13 @@
     pred_part[0] = predicted
     pred_out[...] = pred_part[0, :, cols]
     to_mate.wait_send()
+    for j in range(3):
+        along(j).wait_send()
+
+    @pl.when(y != k)
+    def _():
+        along(3).wait_send()
+
 
     def arrived(slot):
         return copy_to(z_send.at[0], z_in.at[slot], g_send.at[0], g_recv.at[slot], device(0, 0, 0, 1))
@@ -626,13 +667,6 @@
         spot = slice(h * HEAD_DIM, (h + 1) * HEAD_DIM)
         grad_out[:tall, spot] = summed[tall * h : tall * h + tall, :HEAD_DIM]
         grad_out[tall:, spot] = summed[tall * h : tall * h + tall, HEAD_DIM:]
-    for j in range(3):
-        along(j).wait_send()
-
-    @pl.when(y != k)
-    def _():
-        along(3).wait_send()
-
 
 def finish(pred_in, grad_in, pred_o, grad_o):
     pred_o[...] = pred_in[...]
@@ -686,15 +720,18 @@
             pltpu.VMEM((cells, D), BF),
             pltpu.VMEM((4, 8, D), F32),
             pltpu.VMEM((4, 8, D), BF),
-            pltpu.VMEM((8, 8, D), BF),
+            pltpu.VMEM((16, 8, D), BF),
             pltpu.VMEM((D, 256), BF),
-            pltpu.VMEM((4, 8, 256), BF),
-            pltpu.VMEM((16, 8, 256), BF),
+            pltpu.VMEM((4, 16, 256), BF),
+            pltpu.VMEM((8, 16, 256), BF),
             pltpu.VMEM((4, 8, q_dev), F32),
             pltpu.VMEM((4, outs, queries), F32),
             pltpu.VMEM((D, queries), BF),
             pltpu.VMEM((width, queries), F32),
             pltpu.VMEM((256, queries), BF),
+            pltpu.VMEM((width, queries), F32),
+            pltpu.VMEM((width, queries), F32),
+            pltpu.VMEM((width, queries), F32),
             pltpu.VMEM((width // HEAD_DIM, 128, queries), F32),
             pltpu.VMEM((width, queries), BF),
             pltpu.VMEM((4, 3 * deep // 2, 128), BF),
@@ -708,7 +745,7 @@
             dma((3,)),
             dma((3,)),
             dma((31,)),
-            dma((1,)),
+            dma((2,)),
             dma((3,)),
             dma((3,)),
             dma((5,)),

time: 25.5 us -> 24.8 us (0.973)
  Pallas kernels: 24.7 us -> 23.8 us
    pallas_call x1, Pallas kernels: 24.1 us -> 23.1 us  [fused_device(): pl.pallas_call(fused_kernel, out_shape=(pltpu.VMEM((outs, q_dev), F32), p...]
where the time goes in v6:
time: 24.8 us; the launch traced here: 24.4 us
  Pallas kernels  23.8 us (96%)
  between operations  0.64 us (3%)
    pallas_call x1, Pallas kernels, fused_device(): pl.pallas_call(fused_kernel, out_shape=(pltpu.VMEM((outs, q_dev), F32), p...  23.1 us
    pallas_call x1, Pallas kernels, fused_device(): pl.pallas_call(finish, out_shape=(jax.ShapeDtypeStruct((outs, q_dev), F32...  0.65 us

profile of v6, /device:TPU:0, one launch (start us, length us, event | category | flops | bytes accessed | tf_op | source)
XLA Modules:
  0.0 24.4 jit_solution(4289028141785564447)
XLA Ops:
  0.6 23.1 %shard_map.131 = (f32[4,128]{1,0:T(4,128)S(1)}, f32[96,192]{1,0:T(8,128)S(1)}) custom-call(bf16[1024,128]{1,0:T(8,128)(2,1)} %bitcast.8, s32[1,8]{1,0:T(1,128)} %types_h.1, s32[2,1024]{1,0:T(2,128)} %bitcast.9, f32[3,1,128]{2,1,0:T(1,128)} %bitcast.12, f32[4,128]{1,0:T(4,128)} %bitcast.11, bf16[4,128,768]{2,1,0:T(8,128)(2,1)} %type_w_h.1, ...), custom_call_target="tpu_custom_call" | custom-call | tf_op jit(solution)/shard_map/pallas_call | solution.py:697
  23.8 0.7 %shard_map.132 = (f32[4,128]{1,0:T(4,128)}, f32[96,192]{1,0:T(8,128)}) custom-call(f32[4,128]{1,0:T(4,128)S(1)} %get-tuple-element.6.pred_in, f32[96,192]{1,0:T(8,128)S(1)} %get-tuple-element.7.grad_in), custom_call_target="tpu_custom_call" | custom-call | tf_op jit(solution)/shard_map/pallas_call | solution.py:772

commit v7 on v6

--- a/solution.py
+++ b/solution.py
@@ -290,9 +290,9 @@
         for i, (src, dst) in enumerate(
             (
                 (types_h, types),
+                (routes_h, routes),
+                (feats_h, feats),
                 (type_w_h, type_w),
-                (feats_h, feats),
-                (routes_h, routes),
                 (pos_h, pos),
                 (tgt_h, tgt),
                 (out_wt_h, out_wt),
@@ -343,26 +343,23 @@
             src_ref=src, dst_ref=dst, send_sem=send_sem, recv_sem=recv_sem, device_id=peer, device_id_type=MESH
         )
 
-    for load in loads[:3]:
-        load.wait()
-    block = feats.shape[0] // types.shape[1]
-    for b in range(types.shape[1]):
-        pre = mm(feats[b * block : (b + 1) * block, :], type_w[types[0, b]])
-        emb[b * block : (b + 1) * block, :] = jnp.tanh(pre).astype(BF)
-    for load in loads[3:6]:
-        load.wait()
+    loads[1].wait()
     row = lax.broadcasted_iota(jnp.int32, (4 * 8, feats.shape[0]), 0)
     slab = ((row // 16) * 2 + lax.rem(row, 8) // 4) * 2 + lax.rem(row // 8, 2)
     label = (slab * 4 + x) * SN_DEV + lax.rem(row, 4)
     table = (
         jnp.where(routes[0:1, :] == label, 1.0, 0.0) + jnp.where(routes[1:2, :] == label, 1.0, 0.0)
     ).astype(BF)
+    for i in (0, 2, 3):
+        loads[i].wait()
+    block = feats.shape[0] // types.shape[1]
+    for b in range(types.shape[1]):
+        pre = mm(feats[b * block : (b + 1) * block, :], type_w[types[0, b]])
+        emb[b * block : (b + 1) * block, :] = jnp.tanh(pre).astype(BF)
     sums = mm(table, emb[...])
     for o in range(4):
         part[o] = sums[8 * o : 8 * o + 8, :]
         part_b[o] = sums[8 * o : 8 * o + 8, :].astype(BF)
-    both_all[place, 0:3, :] = pos[:, 0, :]
-    both_all[place, 4:8, :] = tgt[...]
 
     def pool_copy(i):
         dh, dy = ((1, 1), (1, 0), (0, 1), (0, 0))[i]
@@ -387,6 +384,10 @@
     def _():
         pl.semaphore_signal(ready, inc=1, device_id=device(0, 0, 1, 0), device_id_type=MESH)
 
+    loads[4].wait()
+    loads[5].wait()
+    both_all[place, 0:3, :] = pos[:, 0, :]
+    both_all[place, 4:8, :] = tgt[...]
     p_copies = []
     quad = ((1, 1), (1, 0), (0, 1))
     for i, (dy, dx) in enumerate(quad):

time: 24.8 us -> 24.7 us (level)
  no operation moved by 1% of the time
where the time goes in v7:
time: 24.7 us; the launch traced here: 24.3 us
  Pallas kernels  23.7 us (96%)
  between operations  0.64 us (3%)
    pallas_call x1, Pallas kernels, fused_device(): pl.pallas_call(fused_kernel, out_shape=(pltpu.VMEM((outs, q_dev), F32), p...  23 us
    pallas_call x1, Pallas kernels, fused_device(): pl.pallas_call(finish, out_shape=(jax.ShapeDtypeStruct((outs, q_dev), F32...  0.65 us

profile of v7, /device:TPU:0, one launch (start us, length us, event | category | flops | bytes accessed | tf_op | source)
XLA Modules:
  0.0 24.3 jit_solution(7109494101463017868)
XLA Ops:
  0.6 23.0 %shard_map.131 = (f32[4,128]{1,0:T(4,128)S(1)}, f32[96,192]{1,0:T(8,128)S(1)}) custom-call(bf16[1024,128]{1,0:T(8,128)(2,1)} %bitcast.8, s32[1,8]{1,0:T(1,128)} %types_h.1, s32[2,1024]{1,0:T(2,128)} %bitcast.9, f32[3,1,128]{2,1,0:T(1,128)} %bitcast.12, f32[4,128]{1,0:T(4,128)} %bitcast.11, bf16[4,128,768]{2,1,0:T(8,128)(2,1)} %type_w_h.1, ...), custom_call_target="tpu_custom_call" | custom-call | tf_op jit(solution)/shard_map/pallas_call | solution.py:698
  23.7 0.7 %shard_map.132 = (f32[4,128]{1,0:T(4,128)}, f32[96,192]{1,0:T(8,128)}) custom-call(f32[4,128]{1,0:T(4,128)S(1)} %get-tuple-element.6.pred_in, f32[96,192]{1,0:T(8,128)S(1)} %get-tuple-element.7.grad_in), custom_call_target="tpu_custom_call" | custom-call | tf_op jit(solution)/shard_map/pallas_call | solution.py:773

commit v8 on v7

--- a/solution.py
+++ b/solution.py
@@ -594,8 +594,9 @@
     deep = D // 8
     tall = deep // 2
     middle = (z == 1) | (z == 2)
-    places = [jnp.where(middle, a, b) for a, b in ((2, 3), (1, 2), (3, 1))]
-    layers = [jnp.where(middle, far_z(a), far_z(b)) for a, b in ((2, 3), (1, 2), (3, 1))] + [z]
+    steps_of = ((1, 2, 3), (2, 1, 2), (3, 3, 1))
+    places = [jnp.where(z == 1, a, jnp.where(z == 2, b, e)) for a, b, e in steps_of]
+    layers = [jnp.where(z == 1, far_z(a), jnp.where(z == 2, far_z(b), far_z(e))) for a, b, e in steps_of] + [z]
 
     def blocks(side, steps):
         slabs = [emb_t[pl.ds(pl.multiple_of((layers[j] * 2 + side) * deep, 16), deep), :] for j in steps]
@@ -622,12 +623,13 @@
         peer = {"cells": layers[j] * 2 + k, "ctx": xx * 2 + y}
         return copy_to(z_send.at[j], z_in.at[slot], g_send.at[j], g_recv.at[slot], peer)
 
-    kept = blocks(k, (0,))
+    kept = blocks(k, (0, 1))
     to_mate.wait_recv()
-    z_send[0] = (kept[0] + y_in[0].astype(F32)).astype(BF)
-    along(0).start()
-    kept = blocks(k, (1, 2, 3))
-    for j in (1, 2):
+    for j in (0, 1):
+        z_send[j] = (kept[j] + y_in[j].astype(F32)).astype(BF)
+        along(j).start()
+    kept = blocks(k, (2, 3))
+    for j in (2,):
         z_send[j] = (kept[j] + y_in[j].astype(F32)).astype(BF)
         along(j).start()
     near = kept[3] + y_in[3].astype(F32)

time: 24.7 us -> 24.7 us (level)
  no operation moved by 1% of the time
where the time goes in v8:
time: 24.7 us; the launch traced here: 24.4 us
  Pallas kernels  23.7 us (96%)
  between operations  0.64 us (3%)
    pallas_call x1, Pallas kernels, fused_device(): pl.pallas_call(fused_kernel, out_shape=(pltpu.VMEM((outs, q_dev), F32), p...  23.1 us
    pallas_call x1, Pallas kernels, fused_device(): pl.pallas_call(finish, out_shape=(jax.ShapeDtypeStruct((outs, q_dev), F32...  0.65 us

profile of v8, /device:TPU:0, one launch (start us, length us, event | category | flops | bytes accessed | tf_op | source)
XLA Modules:
  0.0 24.4 jit_solution(13862041431751491041)
XLA Ops:
  0.6 23.1 %shard_map.131 = (f32[4,128]{1,0:T(4,128)S(1)}, f32[96,192]{1,0:T(8,128)S(1)}) custom-call(bf16[1024,128]{1,0:T(8,128)(2,1)} %bitcast.8, s32[1,8]{1,0:T(1,128)} %types_h.1, s32[2,1024]{1,0:T(2,128)} %bitcast.9, f32[3,1,128]{2,1,0:T(1,128)} %bitcast.12, f32[4,128]{1,0:T(4,128)} %bitcast.11, bf16[4,128,768]{2,1,0:T(8,128)(2,1)} %type_w_h.1, ...), custom_call_target="tpu_custom_call" | custom-call | tf_op jit(solution)/shard_map/pallas_call | solution.py:700
  23.7 0.7 %shard_map.132 = (f32[4,128]{1,0:T(4,128)}, f32[96,192]{1,0:T(8,128)}) custom-call(f32[4,128]{1,0:T(4,128)S(1)} %get-tuple-element.6.pred_in, f32[96,192]{1,0:T(8,128)S(1)} %get-tuple-element.7.grad_in), custom_call_target="tpu_custom_call" | custom-call | tf_op jit(solution)/shard_map/pallas_call | solution.py:775
